TPU v7x, 32 devices: a whole 2x2x4 slice. The times are simulated.
32 devices in a mesh: lemma: 8 (over y, x, core), grp: 4 (over z).
Axes of the slice: x: 2, y: 2, z: 4, core: 2. Of those that a mesh axis runs over, the one named last changes fastest.
Arguments:
- hidden: bfloat16 [64, 64, 1536], P(('lemma', 'grp')), may hold values from -6 to 6
- gain: float32 [1536], replicated, may hold values from 0.3 to 2.1
- weight: bfloat16 [1536, 128], P('grp'), may hold values from -0.15625 to 0.15625
- lemma_emb: bfloat16 [128, 32, 128], P('lemma'), may hold values from -6 to 6
- lemma_len: int32 [128], replicated, may hold values from 8 to 32
- query_len: int32 [64], replicated, may hold values from 16 to 64
- positive: int32 [64], replicated, may hold values from 0 to 127
Outputs:
- loss: float32 [64], P(('lemma', 'grp'))
- hidden_grad: bfloat16 [64, 64, 1536], P(('lemma', 'grp'))
- weight_grad: float32 [1536, 128], P('grp')
- gain_grad: float32 [1536], P('grp')
All inputs are finite; a program needn't handle non-finite values.
Results may differ from a plain program's by a relative error of at most 0.03.
Values may be sent and summed in bfloat16 or wider, within the bound.
A program may use at most 64 MiB of HBM per device.

v0:
```python
import math

import jax
import jax.numpy as jnp
from jax import lax
from jax.sharding import PartitionSpec as P

token_temp = 0.05
state_temp = 0.05
loss_scale = 1024.0
grad_limit = 400.0
norm_eps = 1e-06


def contract_last(left, right):
    return lax.dot_general(
        left, right, (((1,), (1,)), ((), ())), preferred_element_type=jnp.float32
    )


def unit_rows(values):
    scale_rows = lax.rsqrt(jnp.mean(values * values, axis=-1, keepdims=True) + norm_eps)
    return values * scale_rows / math.sqrt(values.shape[-1])


def lemma_terms(queries, keys, key_live, lemma_count, lemma_tok):
    scores = contract_last(queries, keys)
    exp_terms = jnp.exp(scores / token_temp) * key_live[None, :]
    per_lemma = jnp.sum(exp_terms.reshape(queries.shape[0], lemma_count, lemma_tok), axis=2)
    return (exp_terms, per_lemma)


def token_grads(queries, grads, keys, key_live, lemma_count, lemma_tok):
    exp_terms, per_lemma = lemma_terms(queries, keys, key_live, lemma_count, lemma_tok)
    rows = queries.shape[0]
    weights = exp_terms.reshape(rows, lemma_count, lemma_tok) / per_lemma[:, :, None]
    coef = (weights * grads[:, :, None]).reshape(rows, lemma_count * lemma_tok).astype(jnp.bfloat16)
    return jnp.dot(coef, keys, preferred_element_type=jnp.float32)


def state_loss(tok_lse, live_rows, lengths_f, targets, lemma_ids):
    states = live_rows.shape[0]
    similarity = (
        jnp.sum(tok_lse.reshape(states, live_rows.shape[1], -1) * live_rows[:, :, None], axis=1)
        / lengths_f[:, None]
    )
    powers = jnp.exp(similarity / state_temp)
    is_positive = (lemma_ids[None, :] == targets[:, None]).astype(jnp.float32)
    return (similarity, powers, is_positive)


def body(hidden, gain, weight, lemma_emb, lemma_len, query_len, positive):
    states_dev, query_tok, width = hidden.shape
    proj_width = weight.shape[1]
    lemma_dev, lemma_tok = (lemma_emb.shape[0], lemma_emb.shape[1])
    lemma_axis = lax.axis_size("lemma")
    group_axis = lax.axis_size("grp")
    lemma_idx = lax.axis_index("lemma")
    group_idx = lax.axis_index("grp")
    own_rows = states_dev * query_tok
    lemmas_all = lemma_dev * lemma_axis
    in_float = hidden.reshape(own_rows, width).astype(jnp.float32)
    inv_rms = lax.rsqrt(jnp.mean(in_float * in_float, axis=1, keepdims=True) + norm_eps)
    normed = in_float * inv_rms
    scaled = (normed * gain[None, :]).astype(jnp.bfloat16)
    projected = jnp.dot(
        scaled,
        lax.all_gather(weight, "grp", axis=0, tiled=True),
        preferred_element_type=jnp.float32,
    )
    proj_scale = lax.rsqrt(
        jnp.mean(projected * projected, axis=1, keepdims=True) + norm_eps
    ) / math.sqrt(proj_width)
    query_unit = (projected * proj_scale).astype(jnp.bfloat16)
    lemma_unit = unit_rows(lemma_emb.astype(jnp.float32).reshape(-1, proj_width)).astype(
        jnp.bfloat16
    )
    all_live = (jnp.arange(lemma_tok)[None, :] < lemma_len[:, None]).astype(jnp.float32)
    block_start = (lemma_idx * group_axis + group_idx) * states_dev
    all_keys = lax.all_gather(lemma_unit, "lemma", axis=0, tiled=True)
    block_count = 8
    block_lemmas = lemmas_all // block_count
    key_blocks = all_keys.reshape(block_count, block_lemmas * lemma_tok, proj_width)
    live_blocks = all_live.reshape(block_count, block_lemmas * lemma_tok)
    own_len = lax.dynamic_slice_in_dim(query_len, block_start, states_dev)
    own_pos = lax.dynamic_slice_in_dim(positive, block_start, states_dev)
    live_rows = (jnp.arange(query_tok)[None, :] < own_len[:, None]).astype(jnp.float32)
    lengths_f = own_len.astype(jnp.float32)

    def block_lse(items):
        keys, key_live = items
        exp_terms, per_lemma = lemma_terms(query_unit, keys, key_live, block_lemmas, lemma_tok)
        return token_temp * jnp.log(per_lemma)

    tok_lse = lax.map(block_lse, (key_blocks, live_blocks))
    tok_lse = jnp.moveaxis(tok_lse, 0, 1).reshape(own_rows, lemmas_all)
    similarity, powers, is_positive = state_loss(
        tok_lse, live_rows, lengths_f, own_pos, jnp.arange(lemmas_all)
    )
    partition = jnp.sum(powers, axis=1)
    pos_score = jnp.sum(similarity * is_positive, axis=1)
    loss = jnp.log(partition) - pos_score / state_temp
    grad_sim = loss_scale * (powers / partition[:, None] - is_positive) / state_temp
    tok_grad = (grad_sim[:, None, :] * live_rows[:, :, None] / lengths_f[:, None, None]).reshape(
        own_rows, block_count, block_lemmas
    )
    grad_blocks = jnp.moveaxis(tok_grad, 1, 0)

    def add_block(acc, items):
        keys, key_live, grads = items
        return (acc + token_grads(query_unit, grads, keys, key_live, block_lemmas, lemma_tok), None)

    unit_grad, unused = lax.scan(
        add_block,
        jnp.zeros((own_rows, proj_width), jnp.float32),
        (key_blocks, live_blocks, grad_blocks),
    )
    proj_grad = proj_scale * unit_grad - projected * proj_scale**3 * jnp.sum(
        projected * unit_grad, axis=1, keepdims=True
    )
    proj_grad_b = proj_grad.astype(jnp.bfloat16)
    scaled_grad = contract_last(proj_grad_b, lax.all_gather(weight, "grp", axis=0, tiled=True))
    normed_grad = scaled_grad * gain[None, :]
    input_grad = (
        inv_rms * normed_grad
        - in_float * inv_rms**3 * jnp.sum(in_float * normed_grad, axis=1, keepdims=True) / width
    )
    hidden_grad = input_grad.astype(jnp.bfloat16).reshape(states_dev, query_tok, width)
    weight_part = lax.dot_general(
        scaled, proj_grad_b, (((0,), (0,)), ((), ())), preferred_element_type=jnp.float32
    )
    gain_part = jnp.sum(scaled_grad * normed, axis=0)
    weight_sum, gain_sum = (
        lax.psum(weight_part.astype(jnp.bfloat16), "lemma").astype(jnp.float32),
        lax.psum(gain_part.astype(jnp.bfloat16), "lemma").astype(jnp.float32),
    )
    weight_sum, gain_sum = (
        lax.psum_scatter(
            weight_sum.astype(jnp.bfloat16), "grp", scatter_dimension=0, tiled=True
        ).astype(jnp.float32),
        lax.psum_scatter(
            gain_sum.astype(jnp.bfloat16), "grp", scatter_dimension=0, tiled=True
        ).astype(jnp.float32),
    )
    squares = jnp.sum(weight_sum * weight_sum) + jnp.sum(gain_sum * gain_sum)
    total_squares = lax.psum(squares, "grp")
    factor = jnp.minimum(1.0, grad_limit / jnp.sqrt(total_squares + norm_eps))
    return (loss, hidden_grad, weight_sum * factor, gain_sum * factor)


def solution(mesh):
    in_specs = (
        P(("lemma", "grp"), None, None),
        P(),
        P("grp", None),
        P("lemma", None, None),
        P(),
        P(),
        P(),
    )
    out_specs = (P(("lemma", "grp")), P(("lemma", "grp"), None, None), P("grp", None), P("grp"))
    return jax.shard_map(body, mesh=mesh, in_specs=in_specs, out_specs=out_specs, check_vma=False)
```

profile of v0, /device:TPU:0, one launch (start us, length us, event | category | flops | bytes accessed | tf_op | source)
XLA Modules:
  0.0 171.3 jit_solution(15124283781824638418)
XLA Ops:
  7.2 1.1 multiply_reduce_fusion
  8.4 0.8 fusion.28
  9.4 0.2 fusion.21
  9.6 0.6 copy-done.3
  10.2 16.4 %all_gather.8 = bf16[1536,128]{1,0:T(8,128)(2,1)S(1)} all-gather(bf16[384,128]{1,0:T(8,128)(2,1)S(1)} %copy-done.3), channel_id=1, replica_groups=mesh['lemma'=8,'grp'=4] {'grp'}, dimensions={0}, use_global_device_ids=true | all-gather | bytes 491520 | tf_op jit(solution)/shard_map/all_gather | solution.py:68
  26.6 0.2 fusion.19
  26.8 0.3 multiply_reduce_fusion.3
  27.1 0.1 copy.19
  27.3 0.5 copy-done.5
  28.1 0.7 copy-done.7
  28.9 0.6 copy-done.6
  29.8 6.9 %all-gather.2.cloned.1.call-done = bf16[4096,128]{1,0:T(8,128)(2,1)} async-done(((bf16[512,128]{1,0:T(8,128)(2,1)}), bf16[4096,128]{1,0:T(8,128)(2,1)}) %all-gather.2.cloned.1.call-update) | async-done | bytes 1048592 | tf_op jit(solution)/shard_map/all_gather | solution.py:80
  36.7 9.5 %while.21 = (s32[]{:T(128)}, f32[8,128,16]{1,2,0:T(8,128)S(1)}, bf16[8,512,128]{2,1,0:T(8,128)(2,1)}, bf16[128,128]{1,0:T(8,128)(2,1)S(1)}, f32[8,512]{1,0:T(8,128)S(1)}, /*index=5*/s32[]{:T(128)}) while((s32[]{:T(128)}, f32[8,128,16]{1,2,0:T(8,128)S(1)}, bf16[8,512,128]{2,1,0:T(8,128)(2,1)}, bf16[128,128]{1,0:T(8,128)(2,1)S(1)}, ...), condition=%wide.region_5.6_spmd, body=%wide.region_3.5_spmd.sunk | while | flops 16973824 | bytes 194649 | solution.py:95
  36.7 1.1 bitcast_reduce_fusion.3
  37.9 1.1 bitcast_reduce_fusion.3
  39.1 1.1 bitcast_reduce_fusion.3
  40.3 1.1 bitcast_reduce_fusion.3
  41.5 1.1 bitcast_reduce_fusion.3
  42.7 1.1 bitcast_reduce_fusion.3
  43.9 1.1 bitcast_reduce_fusion.3
  45.0 1.1 bitcast_reduce_fusion.3
  46.2 0.1 reshape_reshape.3
  46.3 0.2 multiply_reduce_fusion.1
  46.6 0.2 mul.224
  46.8 0.1 mul.225
  47.0 22.4 %while.22 = (s32[]{:T(128)}, f32[128,128]{1,0:T(8,128)S(1)}, bf16[8,512,128]{2,1,0:T(8,128)(2,1)}, bf16[128,128]{1,0:T(8,128)(2,1)S(1)}, f32[8,512]{1,0:T(8,128)...) while((s32[]{:T(128)}, f32[128,128]{1,0:T(8,128)S(1)}, ...), condition=%wide.region_11.12_spmd.clone, body=%wide.region_9.11_spmd.clone.sunk | while | flops 33916960 | bytes 2029687 | solution.py:113
  47.0 1.1 fusion.60
  48.1 0.4 fusion.61
  48.6 1.1 convolution_add_fusion.2
  49.8 1.1 fusion.60
  50.9 0.4 fusion.61
  51.4 1.1 convolution_add_fusion.2
  52.6 1.1 fusion.60
  53.7 0.4 fusion.61
  54.2 1.1 convolution_add_fusion.2
  55.4 1.1 fusion.60
  56.6 0.4 fusion.61
  57.1 1.1 convolution_add_fusion.2
  58.2 1.1 fusion.60
  59.4 0.4 fusion.61
  59.9 1.1 convolution_add_fusion.2
  61.0 1.1 fusion.60
  62.2 0.4 fusion.61
  62.7 1.1 convolution_add_fusion.2
  63.8 1.1 fusion.60
  65.0 0.4 fusion.61
  65.5 1.1 convolution_add_fusion.2
  66.7 1.1 fusion.60
  67.8 0.4 fusion.61
  68.3 1.1 convolution_add_fusion.2
  69.6 1.0 convolution_convert_fusion
  70.7 0.6 copy-done.8
  71.4 0.6 dynamic-slice
  72.6 0.4 fusion.20
  73.1 11.7 %all-reduce = bf16[1536]{0:T(1024)(128)(2,1)S(1)} all-reduce(bf16[1536]{0:T(1024)(128)(2,1)S(1)} %get-tuple-element.119), channel_id=3, replica_groups=mesh['lemma'=8,'grp'=4] {'grp'}, use_global_device_ids=true, to_apply=%region_19.20.clone | all-reduce | flops 1536 | bytes 6144
  84.9 11.8 %psum.25 = bf16[384]{0:T(512)(128)(2,1)S(1)} all-reduce(bf16[384]{0:T(512)(128)(2,1)S(1)} %dynamic-slice.1), channel_id=1, replica_groups=mesh['lemma'=8,'grp'=4] {'lemma'}, use_global_device_ids=true, to_apply=%region_18.19 | all-reduce | flops 384 | bytes 1536 | tf_op jit(solution)/shard_map/psum | solution.py:135
  96.7 1.1 fusion.25
  97.8 0.6 fusion.31
  98.4 48.8 %all-reduce.3.cloned.1.call-done = bf16[384,128]{1,0:T(8,128)(2,1)} async-done(((bf16[384,128]{1,0:T(8,128)(2,1)}), bf16[384,128]{1,0:T(8,128)(2,1)}) %all-reduce.3.cloned.1.call-update) | async-done | bytes 98320 | tf_op jit(solution)/shard_map/psum | solution.py:134
  147.2 1.6 fusion.29
  150.1 0.5 multiply_subtract_fusion
  150.6 12.2 %psum.23 = f32[]{:T(128)} all-reduce(f32[]{:T(128)S(6)} %add.73), channel_id=1, replica_groups=mesh['lemma'=8,'grp'=4] {'grp'}, use_global_device_ids=true, to_apply=%region_21.22 | all-reduce | flops 1 | bytes 8 | tf_op jit(solution)/shard_map/psum | solution.py:146
  163.5 0.6 convert_multiply_fusion.3
  164.0 0.7 convert_multiply_fusion.1
  (88 shorter events, 2.2 us)
Async XLA Ops:
  7.2 1.3 copy-start.1
  7.2 2.2 %copy-start = (bf16[2,64,1536]{2,1,0:T(8,128)(2,1)S(1)}, bf16[2,64,1536]{2,1,0:T(8,128)(2,1)}, u32[]{:S(2)}) copy-start(bf16[2,64,1536]{2,1,0:T(8,128)(2,1)} %param.11) | copy-start | bytes 1179652
  7.2 29.5 %all-gather.2.cloned.1.call-start = ((), (), s32[]{:S(2)}) async-start(), calls=%async_computation.1 | async-start | bytes 1179648 | tf_op jit(solution)/shard_map/all_gather | solution.py:80
  9.3 88.5 %reduce-scatter.2.cloned.1.call-start = ((), (), s32[]{:S(2)}) async-start(), calls=%async_computation.2 | async-start | bytes 491520 | tf_op jit(solution)/shard_map/reduce_scatter | solution.py:138
  9.3 0.9 copy-start.3
  10.2 16.4 %copy-start.4 = (f32[1536]{0:T(1024)S(1)}, f32[1536]{0:T(1024)}, u32[]{:S(2)}) copy-start(f32[1536]{0:T(1024)} %param.12) | copy-start | bytes 18436
  27.1 0.7 copy-start.5
  28.1 0.7 copy-start.7
  28.8 0.7 copy-start.6
  70.7 76.5 %all-reduce.3.cloned.1.call-start = ((), (), s32[]{:S(2)}) async-start(), calls=%async_computation.3 | async-start | bytes 196608 | tf_op jit(solution)/shard_map/psum | solution.py:134
  70.7 0.7 copy-start.8
  147.2 16.9 %copy-start.2 = (bf16[384,128]{1,0:T(8,128)(2,1)S(1)}, bf16[384,128]{1,0:T(8,128)(2,1)}, u32[]{:S(2)}) copy-start(bf16[384,128]{1,0:T(8,128)(2,1)} %all-reduce.3.cloned.1.call-done) | copy-start | bytes 294916
Sparse Core Ops, SparseCore 0:
  10.5 26.1 all-gather.1
  70.8 20.6 reduce-scatter.1
  97.9 49.1 all-reduce.2
where the time goes:
time: 172 us; the launch traced here: 171 us
  waiting for transfers between devices  55.7 us (32%)
  blocking collectives  52 us (30%)
  matrix products  28.9 us (17%)
  between operations  16.6 us (10%)
  other arithmetic  11.7 us (7%)
  local copies, waits for them, and re-layouts  5.41 us (3%)
    psum x1, waiting for transfers between devices, body(): lax.psum(weight_part.astype(jnp.bfloat16), 'lemma').astype(jnp.float32)  48.8 us
    dot_general x17, matrix products, contract_last(): lax.dot_general(left, right, (((1,), (1,)), ((), ())), preferred_element_...  18.4 us
    all_gather x1, blocking collectives, body(): lax.all_gather(weight, 'grp', axis=0, tiled=True)  16.4 us
    psum x1, blocking collectives, body(): total_squares = lax.psum(squares, 'grp')  12.2 us
    psum x1, blocking collectives, body(): lax.psum(gain_part.astype(jnp.bfloat16), 'lemma').astype(jnp.float32)  11.8 us
    unnamed x1, blocking collectives  11.7 us
    dot_general x8, matrix products, token_grads(): return jnp.dot(coef, keys, preferred_element_type=jnp.float32)  9.18 us
    all_gather x1, waiting for transfers between devices, body(): all_keys = lax.all_gather(lemma_unit, 'lemma', axis=0, tiled=True)  6.88 us
  transfers between devices with their start and end apart: 3, of which 2 were waited for; matrix products, arithmetic and copies ran while one was open for 3% of the time, Pallas kernels for 0%

commit v1 on v0

--- a/solution.py
+++ b/solution.py
@@ -1,8 +1,11 @@
+import functools
 import math
 
 import jax
 import jax.numpy as jnp
 from jax import lax
+from jax.experimental import pallas as pl
+from jax.experimental.pallas import tpu as pltpu
 from jax.sharding import PartitionSpec as P
 
 token_temp = 0.05
@@ -148,6 +151,344 @@
     return (loss, hidden_grad, weight_sum * factor, gain_sum * factor)
 
 
+NT = (((1,), (1,)), ((), ()))
+MESH = pl.DeviceIdType.MESH
+
+
+def fused_kernel(
+    lemma_axis, group_axis, lemma_dev, lemma_tok, states_dev, query_tok,
+    hidden_ref, gain_ref, weight_ref, emb_ref, len_ref, qlen_ref, pos_ref,
+    loss_ref, hgrad_ref, wgrad_ref, ggrad_ref,
+    hid, emb, hout, w_all, keys, live, powers_b, scaled_b, scaled_t,
+    part, pair_in, half, chip_in, quarter, grp_in, raw, sq,
+    local_sem, w_send, w_recv, wf_send, wf_recv, k_send, k_recv, kf_send, kf_recv,
+    p_sem, c_send, c_recv, g_send, g_recv, a_send, a_recv, s_send, s_recv,
+):
+    chips = lemma_axis // 2
+    me, grp = lax.axis_index("lemma"), lax.axis_index("grp")
+    chip, core = me // 2, lax.rem(me, 2)
+    pair = chip * 2 + (1 - core)
+    rows, width = hid.shape
+    proj_width = weight_ref.shape[1]
+    wrows = weight_ref.shape[0]
+    hrows = wrows // 2
+    block_tok = lemma_dev * lemma_tok
+    lemmas_all = lemma_dev * lemma_axis
+
+    def chip_peer(step):
+        return lax.rem(chip + step, chips) * 2 + core
+
+    def chip_from(step):
+        return lax.rem(chip + chips - step, chips) * 2 + core
+
+    def grp_peer(step):
+        return lax.rem(grp + step, group_axis)
+
+    def grp_from(step):
+        return lax.rem(grp + group_axis - step, group_axis)
+
+    def remote(src, dst, send_sem, recv_sem, to_lemma, to_grp):
+        return pltpu.make_async_remote_copy(
+            src_ref=src, dst_ref=dst, send_sem=send_sem, recv_sem=recv_sem,
+            device_id=(to_lemma, to_grp), device_id_type=MESH,
+        )
+
+    emb_copy = pltpu.make_async_copy(emb_ref, emb, local_sem.at[0])
+    hid_copy = pltpu.make_async_copy(hidden_ref, hid, local_sem.at[1])
+    w_copy = pltpu.make_async_copy(weight_ref, w_all.at[grp], local_sem.at[2])
+    emb_copy.start()
+    w_copy.start()
+    hid_copy.start()
+
+    barrier = pltpu.get_barrier_semaphore()
+    for step in range(1, lemma_axis):
+        pl.semaphore_signal(
+            barrier, inc=1, device_id=(lax.rem(me + step, lemma_axis), grp), device_id_type=MESH
+        )
+    for step in range(1, group_axis):
+        pl.semaphore_signal(barrier, inc=1, device_id=(me, grp_peer(step)), device_id_type=MESH)
+
+    emb_copy.wait()
+    tokens = emb[...].astype(jnp.float32)
+    token_scale = lax.rsqrt(
+        jnp.mean(tokens * tokens, axis=1, keepdims=True) + norm_eps
+    ) / math.sqrt(proj_width)
+    keys[me] = (tokens * token_scale).astype(jnp.bfloat16)
+    w_copy.wait()
+    pl.semaphore_wait(barrier, lemma_axis - 1 + group_axis - 1)
+
+    my_half = pl.ds(pl.multiple_of(core * hrows, hrows), hrows)
+    w_out = []
+    for step in range(1, group_axis):
+        src = w_all.at[grp, my_half]
+        copy = remote(src, src, w_send.at[step], w_recv.at[step], me, grp_peer(step))
+        copy.start()
+        w_out.append(copy)
+    k_out = []
+    for step in range(1, chips):
+        copy = remote(
+            keys.at[me], keys.at[me], k_send.at[step], k_recv.at[step], chip_peer(step), grp
+        )
+        copy.start()
+        k_out.append(copy)
+    kf_out = [remote(keys.at[me], keys.at[me], kf_send.at[0], kf_recv.at[0], pair, grp)]
+    kf_out[0].start()
+
+    token_row = lax.broadcasted_iota(jnp.int32, (block_tok, lemmas_all), 0)
+    lemma_col = lax.broadcasted_iota(jnp.int32, (block_tok, lemmas_all), 1)
+    alive = lax.rem(token_row, lemma_tok) < len_ref[...]
+    for block in range(lemma_axis):
+        member = lemma_col == token_row // lemma_tok + block * lemma_dev
+        live[block] = jnp.where(member & alive, 1.0, 0.0).astype(jnp.bfloat16)
+
+    hid_copy.wait()
+    in_float = hid[...].astype(jnp.float32)
+    inv_rms = lax.rsqrt(jnp.mean(in_float * in_float, axis=1, keepdims=True) + norm_eps)
+    scaled = (in_float * inv_rms * gain_ref[...]).astype(jnp.bfloat16)
+    scaled_b[...] = scaled
+    scaled_t[...] = scaled.T
+
+    wf_out = []
+    for step in range(1, group_axis):
+        dst = w_all.at[grp_from(step), my_half]
+        remote(dst, dst, w_send.at[step], w_recv.at[step], me, grp_peer(step)).wait_recv()
+        copy = remote(dst, dst, wf_send.at[step], wf_recv.at[step], pair, grp)
+        copy.start()
+        wf_out.append(copy)
+    for step in range(1, chips):
+        dst = keys.at[chip_from(step)]
+        remote(dst, dst, k_send.at[step], k_recv.at[step], chip_peer(step), grp).wait_recv()
+        copy = remote(dst, dst, kf_send.at[step], kf_recv.at[step], pair, grp)
+        copy.start()
+        kf_out.append(copy)
+    other_half = pl.ds(pl.multiple_of((1 - core) * hrows, hrows), hrows)
+    for step in range(1, group_axis):
+        dst = w_all.at[grp_from(step), other_half]
+        remote(dst, dst, wf_send.at[step], wf_recv.at[step], pair, grp).wait_recv()
+
+    weight = w_all[...].reshape(width, proj_width)
+    projected = jnp.dot(scaled_b[...], weight, preferred_element_type=jnp.float32)
+    proj_scale = lax.rsqrt(
+        jnp.mean(projected * projected, axis=1, keepdims=True) + norm_eps
+    ) / math.sqrt(proj_width)
+    query_unit = (projected * proj_scale).astype(jnp.bfloat16)
+
+    def first_pass(block, total):
+        scores = lax.dot_general(
+            query_unit, keys[block], NT, preferred_element_type=jnp.float32
+        )
+        exp_terms = jnp.exp(scores * (1.0 / token_temp)).astype(jnp.bfloat16)
+        powers_b[block] = exp_terms
+        return total + jnp.dot(exp_terms, live[block], preferred_element_type=jnp.float32)
+
+    total = first_pass(me, jnp.zeros((rows, lemmas_all), jnp.float32))
+    for step in range(1, chips):
+        total = first_pass(chip_from(step), total)
+    for step in range(chips):
+        block = lax.rem(chip + chips - step, chips) * 2 + (1 - core)
+        dst = keys.at[block]
+        remote(dst, dst, kf_send.at[step], kf_recv.at[step], pair, grp).wait_recv()
+        total = first_pass(block, total)
+
+    tok_lse = token_temp * jnp.log(total)
+    first_state = (me * group_axis + grp) * states_dev
+    ratios = []
+    for state in range(states_dev):
+        length = qlen_ref[first_state + state]
+        target = pos_ref[first_state + state]
+        length_f = jnp.full((1, lemmas_all), length, jnp.int32).astype(jnp.float32)
+        span = slice(state * query_tok, (state + 1) * query_tok)
+        row_ids = lax.broadcasted_iota(jnp.int32, (query_tok, lemmas_all), 0)
+        live_rows = jnp.where(row_ids < length, 1.0, 0.0)
+        similarity = jnp.sum(tok_lse[span] * live_rows, axis=0, keepdims=True) / length_f
+        powers = jnp.exp(similarity / state_temp)
+        lemma_ids = lax.broadcasted_iota(jnp.int32, (1, lemmas_all), 1)
+        is_positive = jnp.where(lemma_ids == target, 1.0, 0.0)
+        partition = jnp.sum(powers, axis=1, keepdims=True)
+        pos_score = jnp.sum(similarity * is_positive, axis=1, keepdims=True)
+        loss = jnp.log(partition) - pos_score / state_temp
+        loss_ref[state] = jnp.sum(loss)
+        grad_sim = loss_scale * (powers / partition - is_positive) / state_temp
+        ratios.append(live_rows * (grad_sim / length_f) / total[span])
+    ratio = jnp.concatenate(ratios, axis=0).astype(jnp.bfloat16)
+
+    unit_grad = jnp.zeros((rows, proj_width), jnp.float32)
+    for block in range(lemma_axis):
+        spread = lax.dot_general(ratio, live[block], NT, preferred_element_type=jnp.float32)
+        coef = (powers_b[block].astype(jnp.float32) * spread).astype(jnp.bfloat16)
+        unit_grad += jnp.dot(coef, keys[block], preferred_element_type=jnp.float32)
+    proj_grad = proj_scale * unit_grad - projected * (
+        proj_scale * proj_scale * proj_scale
+    ) * jnp.sum(projected * unit_grad, axis=1, keepdims=True)
+    proj_grad_b = proj_grad.astype(jnp.bfloat16)
+
+    weight_part = jnp.dot(scaled_t[...], proj_grad_b, preferred_element_type=jnp.float32)
+    piece = wrows // lemma_axis
+    for group in range(group_axis):
+        for owner in range(lemma_axis):
+            start = group * wrows + owner * piece
+            part[owner % 2, owner // 2, group] = weight_part[start : start + piece].astype(
+                jnp.bfloat16
+            )
+    pair_copy = remote(part.at[1 - core], pair_in, p_sem.at[0], p_sem.at[1], pair, grp)
+    pair_copy.start()
+    pair_copy.wait()
+    half[...] = (part[core].astype(jnp.float32) + pair_in[...].astype(jnp.float32)).astype(
+        jnp.bfloat16
+    )
+    c_out = []
+    for step in range(1, chips):
+        copy = remote(
+            half.at[lax.rem(chip + step, chips)], chip_in.at[step - 1],
+            c_send.at[step], c_recv.at[step], chip_peer(step), grp,
+        )
+        copy.start()
+        c_out.append(copy)
+
+    scaled_grad = lax.dot_general(
+        proj_grad_b, w_all[...].reshape(width, proj_width), NT, preferred_element_type=jnp.float32
+    )
+    row_dot = jnp.sum(projected * proj_grad_b.astype(jnp.float32), axis=1, keepdims=True)
+    hout[...] = (
+        inv_rms * (scaled_grad * gain_ref[...])
+        - hid[...].astype(jnp.float32) * (inv_rms * inv_rms * row_dot / width)
+    ).astype(jnp.bfloat16)
+    hout_copy = pltpu.make_async_copy(hout, hgrad_ref, local_sem.at[3])
+    hout_copy.start()
+
+    for copy in c_out:
+        copy.wait()
+    chip_sum = half[chip].astype(jnp.float32)
+    for step in range(1, chips):
+        chip_sum += chip_in[step - 1].astype(jnp.float32)
+    quarter[...] = chip_sum.astype(jnp.bfloat16)
+    g_out = []
+    for step in range(1, group_axis):
+        copy = remote(
+            quarter.at[grp_peer(step)], grp_in.at[step - 1],
+            g_send.at[step], g_recv.at[step], me, grp_peer(step),
+        )
+        copy.start()
+        g_out.append(copy)
+    for copy in g_out:
+        copy.wait()
+    grp_sum = quarter[grp].astype(jnp.float32)
+    for step in range(1, group_axis):
+        grp_sum += grp_in[step - 1].astype(jnp.float32)
+    raw[me] = grp_sum.astype(jnp.bfloat16)
+    a_out = []
+    for step in range(1, lemma_axis):
+        copy = remote(
+            raw.at[me], raw.at[me], a_send.at[step], a_recv.at[step],
+            lax.rem(me + step, lemma_axis), grp,
+        )
+        copy.start()
+        a_out.append(copy)
+    for step in range(1, lemma_axis):
+        dst = raw.at[lax.rem(me + lemma_axis - step, lemma_axis)]
+        remote(dst, dst, a_send.at[step], a_recv.at[step], me, grp_peer(1)).wait_recv()
+
+    weight_raw = raw[...].reshape(wrows, proj_width).astype(jnp.float32)
+    ones = jnp.ones((8, proj_width), jnp.float32)
+    own_gain = gain_ref[:, pl.ds(pl.multiple_of(grp * wrows, 128), wrows)]
+    gain_raw = lax.dot_general(
+        ones, w_all[grp].astype(jnp.float32) * weight_raw, NT,
+        preferred_element_type=jnp.float32, precision=lax.Precision.HIGHEST,
+    )[:1] / own_gain
+    squares = jnp.sum(weight_raw * weight_raw) + jnp.sum(gain_raw * gain_raw)
+    sq[grp] = jnp.full((8, 128), squares, jnp.float32)
+    s_out = []
+    for step in range(1, group_axis):
+        copy = remote(
+            sq.at[grp], sq.at[grp], s_send.at[step], s_recv.at[step], me, grp_peer(step)
+        )
+        copy.start()
+        s_out.append(copy)
+    for step in range(1, group_axis):
+        dst = sq.at[grp_from(step)]
+        remote(dst, dst, s_send.at[step], s_recv.at[step], me, grp_peer(step)).wait_recv()
+    squares_all = sq[0, :1, :]
+    for group in range(1, group_axis):
+        squares_all += sq[group, :1, :]
+    factor = jnp.minimum(1.0, grad_limit / jnp.sqrt(squares_all + norm_eps))
+    wgrad_ref[...] = weight_raw * factor
+    ggrad_ref[...] = gain_raw * factor[:, :1]
+
+    for copy in w_out + k_out + wf_out + kf_out + a_out + s_out:
+        copy.wait_send()
+    hout_copy.wait()
+
+
+def fused_body(hidden, gain, weight, lemma_emb, lemma_len, query_len, positive):
+    states_dev, query_tok, width = hidden.shape
+    wrows, proj_width = weight.shape
+    lemma_dev, lemma_tok = lemma_emb.shape[:2]
+    lemma_axis, group_axis = lax.axis_size("lemma"), lax.axis_size("grp")
+    chips = lemma_axis // 2
+    rows, block_tok = states_dev * query_tok, lemma_dev * lemma_tok
+    piece = wrows // lemma_axis
+    lemmas_all = lemma_dev * lemma_axis
+    vmem = pl.BlockSpec(memory_space=pltpu.VMEM)
+    smem = pl.BlockSpec(memory_space=pltpu.SMEM)
+    hbm = pl.BlockSpec(memory_space=pl.ANY)
+    sem = pltpu.SemaphoreType.DMA
+    bf16, f32 = jnp.bfloat16, jnp.float32
+    outs = pl.pallas_call(
+        functools.partial(
+            fused_kernel, lemma_axis, group_axis, lemma_dev, lemma_tok, states_dev, query_tok
+        ),
+        out_shape=(
+            jax.ShapeDtypeStruct((states_dev,), f32),
+            jax.ShapeDtypeStruct((rows, width), bf16),
+            jax.ShapeDtypeStruct((wrows, proj_width), f32),
+            jax.ShapeDtypeStruct((1, wrows), f32),
+        ),
+        in_specs=[hbm, vmem, hbm, hbm, vmem, smem, smem],
+        out_specs=(smem, hbm, vmem, vmem),
+        scratch_shapes=[
+            pltpu.VMEM((rows, width), bf16),
+            pltpu.VMEM((block_tok, proj_width), bf16),
+            pltpu.VMEM((rows, width), bf16),
+            pltpu.VMEM((group_axis, wrows, proj_width), bf16),
+            pltpu.VMEM((lemma_axis, block_tok, proj_width), bf16),
+            pltpu.VMEM((lemma_axis, block_tok, lemmas_all), bf16),
+            pltpu.VMEM((lemma_axis, rows, block_tok), bf16),
+            pltpu.VMEM((rows, width), bf16),
+            pltpu.VMEM((width, rows), bf16),
+            pltpu.VMEM((2, chips, group_axis, piece, proj_width), bf16),
+            pltpu.VMEM((chips, group_axis, piece, proj_width), bf16),
+            pltpu.VMEM((chips, group_axis, piece, proj_width), bf16),
+            pltpu.VMEM((chips - 1, group_axis, piece, proj_width), bf16),
+            pltpu.VMEM((group_axis, piece, proj_width), bf16),
+            pltpu.VMEM((group_axis - 1, piece, proj_width), bf16),
+            pltpu.VMEM((lemma_axis, piece, proj_width), bf16),
+            pltpu.VMEM((group_axis, 8, 128), f32),
+            sem((4,)),
+            sem((group_axis,)), sem((group_axis,)), sem((group_axis,)), sem((group_axis,)),
+            sem((chips,)), sem((chips,)), sem((chips,)), sem((chips,)),
+            sem((2,)),
+            sem((chips,)), sem((chips,)),
+            sem((group_axis,)), sem((group_axis,)),
+            sem((lemma_axis,)), sem((lemma_axis,)),
+            sem((group_axis,)), sem((group_axis,)),
+        ],
+        compiler_params=pltpu.CompilerParams(
+            collective_id=0, has_side_effects=True, vmem_limit_bytes=48 * 1024 * 1024
+        ),
+        cost_estimate=pl.CostEstimate(
+            flops=2 * rows * proj_width * (3 * width + 4 * block_tok * lemma_axis),
+            bytes_accessed=4 * rows * width * 2,
+            transcendentals=rows * block_tok * lemma_axis,
+        ),
+    )(
+        hidden.reshape(rows, width), gain.reshape(1, width), weight,
+        lemma_emb.reshape(block_tok, proj_width), lemma_len.reshape(1, lemmas_all),
+        query_len, positive,
+    )
+    loss, hidden_grad, weight_grad, gain_grad = outs
+    return (loss, hidden_grad.reshape(hidden.shape), weight_grad, gain_grad.reshape(wrows))
+
+
 def solution(mesh):
     in_specs = (
         P(("lemma", "grp"), None, None),
@@ -159,4 +500,13 @@
         P(),
     )
     out_specs = (P(("lemma", "grp")), P(("lemma", "grp"), None, None), P("grp", None), P("grp"))
-    return jax.shard_map(body, mesh=mesh, in_specs=in_specs, out_specs=out_specs, check_vma=False)
+
+    def run(hidden, gain, weight, *rest):
+        rows = weight.shape[0] // mesh.shape["grp"]
+        tiled = rows % (16 * mesh.shape["lemma"]) == 0 and rows % 128 == 0
+        chosen = fused_body if tiled else body
+        return jax.shard_map(
+            chosen, mesh=mesh, in_specs=in_specs, out_specs=out_specs, check_vma=False
+        )(hidden, gain, weight, *rest)
+
+    return run

time: 172 us -> 43.6 us (0.25)
  waiting for transfers between devices: 55.7 us -> 0 us
  blocking collectives: 52 us -> 0 us
  Pallas kernels: 0 us -> 36.7 us
  matrix products: 28.9 us -> 0 us
  between operations: 16.6 us -> 0.69 us
  other arithmetic: 11.7 us -> 0.6 us
    psum x1 -> x0, waiting for transfers between devices: 48.8 us -> none  [body(): lax.psum(weight_part.astype(jnp.bfloat16), 'lemma').astype(jnp.float32)]
    pallas_call x0 -> x1, Pallas kernels: none -> 36.7 us  [fused_body(): pl.pallas_call(functools.partial(fused_kernel, lemma_axis, group_axis, le...]
    dot_general x27 -> x0, matrix products: 28.9 us -> none  [the longest x17 18.4 us: contract_last(): lax.dot_general(left, right, (((1,), (1,)), ((), ())), preferred_element_...]
    psum x2 -> x0, blocking collectives: 24 us -> none  [the longest x1 12.2 us: body(): total_squares = lax.psum(squares, 'grp')]
    all_gather x1 -> x0, blocking collectives: 16.4 us -> none  [body(): lax.all_gather(weight, 'grp', axis=0, tiled=True)]
    unnamed x1 -> x0, blocking collectives: 11.7 us -> none
    all_gather x1 -> x0, waiting for transfers between devices: 6.88 us -> none  [body(): all_keys = lax.all_gather(lemma_unit, 'lemma', axis=0, tiled=True)]
    reduce_sum x7 -> x0, other arithmetic: 3.78 us -> none  [the longest x2 2.22 us: body(): squares = jnp.sum(weight_sum * weight_sum) + jnp.sum(gain_sum * gain_sum)]
  transfers between devices with their start and end apart: 3 -> 0, of which waited for: 2 -> 0; matrix products, arithmetic and copies ran while one was open for 3% -> 0% of each run, Pallas kernels for 0% -> 0%
where the time goes in v1:
time: 43.6 us; the launch traced here: 43.4 us
  Pallas kernels  36.7 us (84%)
  local copies, waits for them, and re-layouts  5.45 us (12%)
  between operations  0.69 us (2%)
  other arithmetic  0.6 us (1%)
    pallas_call x1, Pallas kernels, fused_body(): pl.pallas_call(functools.partial(fused_kernel, lemma_axis, group_axis, le...  36.7 us
    unnamed x15, local copies, waits for them, and re-layouts  4.73 us

profile of v1, /device:TPU:0, one launch (start us, length us, event | category | flops | bytes accessed | tf_op | source)
XLA Modules:
  0.0 43.4 jit_solution(9031266263397885621)
XLA Ops:
  0.6 0.0 copy-start.3
  0.6 0.0 copy-start.4
  0.7 0.0 copy-start.5
  0.7 0.7 %reshape.27.gain_ref = f32[1,1536]{1,0:T(1,128)S(1)} reshape(f32[1536]{0:T(1024)} %param.8) | data formatting | bytes 12288 | tf_op jit(solution)/shard_map/reshape | solution.py:484
  1.4 0.0 copy-done.3
  1.4 0.0 copy-done.4
  1.4 0.0 copy-done.5
  1.4 0.0 copy-start
  1.4 1.0 %copy-done = bf16[2,64,1536]{2,1,0:T(8,128)(2,1)S(1)} copy-done((bf16[2,64,1536]{2,1,0:T(8,128)(2,1)S(1)}, bf16[2,64,1536]{2,1,0:T(8,128)(2,1)}, u32[]{:S(2)}) %copy-start) | copy-done | bytes 393240
  2.4 0.0 copy-start.1
  2.4 0.9 %copy-done.1 = bf16[16,32,128]{2,1,0:T(8,128)(2,1)S(1)} copy-done((bf16[16,32,128]{2,1,0:T(8,128)(2,1)S(1)}, bf16[16,32,128]{2,1,0:T(8,128)(2,1)}, u32[]{:S(2)}) %copy-start.1) | copy-done | bytes 131096
  3.3 0.0 copy-start.2
  3.3 0.9 %copy-done.2 = bf16[384,128]{1,0:T(8,128)(2,1)S(1)} copy-done((bf16[384,128]{1,0:T(8,128)(2,1)S(1)}, bf16[384,128]{1,0:T(8,128)(2,1)}, u32[]{:S(2)}) %copy-start.2) | copy-done | bytes 98328
  4.2 36.7 %shard_map.102 = (f32[2]{0:T(128)S(1)}, bf16[128,1536]{1,0:T(8,128)(2,1)S(1)}, f32[384,128]{1,0:T(8,128)S(1)}, f32[1,384]{1,0:T(1,128)S(1)}) custom-call(bf16[128,1536]{1,0:T(8,128)(2,1)S(1)} %bitcast.5, f32[1,1536]{1,0:T(1,128)S(1)} %reshape.27.gain_ref, bf16[384,128]{1,0:T(8,128)(2,1)S(1)} %copy-done.2, bf16[512,128]{1,0:T(8,128)(2,1)S(1)} %bitcast.6, ...), custom_call_target="tpu_custom_call" | custom-call | flops 687865856 | bytes 1572864 | tf_op jit(solution)/shard_map/pallas_call | solution.py:436
  40.9 0.6 %reduce = f32[384]{0:T(512)} reduce(f32[1,384]{1,0:T(1,128)S(1)} %get-tuple-element.11, f32[]{:T(128)} %constant.1), dimensions={0}, to_apply=%get-tuple-element.11.reduce_sub_computation | reduce | bytes 3076 | tf_op jit(solution)/shard_map/pallas_call | solution.py:436
  41.5 0.5 %copy.14 = f32[2]{0:T(128)} copy(f32[2]{0:T(128)S(1)} %get-tuple-element.16) | data formatting | bytes 16
  42.0 0.7 %copy.15 = bf16[2,64,1536]{2,1,0:T(8,128)(2,1)} copy(bf16[2,64,1536]{2,1,0:T(8,128)(2,1)S(1)} %bitcast.4) | data formatting | bytes 786432
  42.7 0.7 %copy.16 = f32[384,128]{1,0:T(8,128)} copy(f32[384,128]{1,0:T(8,128)S(1)} %get-tuple-element.18) | data formatting | bytes 393216
Async XLA Ops:
  0.6 0.8 %copy-start.3 = (s32[128]{0:T(128)S(1)}, s32[128]{0:T(128)}, u32[]{:S(2)}) copy-start(s32[128]{0:T(128)} %param.11) | copy-start | bytes 1540
  0.6 0.7 %copy-start.4 = (s32[64]{0:T(128)S(1)}, s32[64]{0:T(128)}, u32[]{:S(2)}) copy-start(s32[64]{0:T(128)} %qlen_ref.1) | copy-start | bytes 772
  0.7 0.7 %copy-start.5 = (s32[64]{0:T(128)S(1)}, s32[64]{0:T(128)}, u32[]{:S(2)}) copy-start(s32[64]{0:T(128)} %pos_ref.1) | copy-start | bytes 772
  1.4 1.0 %copy-start = (bf16[2,64,1536]{2,1,0:T(8,128)(2,1)S(1)}, bf16[2,64,1536]{2,1,0:T(8,128)(2,1)}, u32[]{:S(2)}) copy-start(bf16[2,64,1536]{2,1,0:T(8,128)(2,1)} %param.7) | copy-start | bytes 1179652
  2.4 0.9 %copy-start.1 = (bf16[16,32,128]{2,1,0:T(8,128)(2,1)S(1)}, bf16[16,32,128]{2,1,0:T(8,128)(2,1)}, u32[]{:S(2)}) copy-start(bf16[16,32,128]{2,1,0:T(8,128)(2,1)} %param.10) | copy-start | bytes 393220
  3.3 0.9 %copy-start.2 = (bf16[384,128]{1,0:T(8,128)(2,1)S(1)}, bf16[384,128]{1,0:T(8,128)(2,1)}, u32[]{:S(2)}) copy-start(bf16[384,128]{1,0:T(8,128)(2,1)} %weight_ref.1) | copy-start | bytes 294916

commit v2 on v1

--- a/solution.py
+++ b/solution.py
@@ -169,6 +169,7 @@
     chip, core = me // 2, lax.rem(me, 2)
     pair = chip * 2 + (1 - core)
     rows, width = hid.shape
+    gain_row = gain_ref[...].reshape(1, width)
     proj_width = weight_ref.shape[1]
     wrows = weight_ref.shape[0]
     hrows = wrows // 2
@@ -234,17 +235,19 @@
     kf_out = [remote(keys.at[me], keys.at[me], kf_send.at[0], kf_recv.at[0], pair, grp)]
     kf_out[0].start()
 
-    token_row = lax.broadcasted_iota(jnp.int32, (block_tok, lemmas_all), 0)
-    lemma_col = lax.broadcasted_iota(jnp.int32, (block_tok, lemmas_all), 1)
-    alive = lax.rem(token_row, lemma_tok) < len_ref[...]
+    token_of = lax.broadcasted_iota(
+        jnp.int32, (block_tok, lemmas_all), 0
+    ) - lemma_tok * lax.broadcasted_iota(jnp.int32, (block_tok, lemmas_all), 1)
+    lengths = jnp.minimum(len_ref[...].reshape(1, lemmas_all), lemma_tok)
     for block in range(lemma_axis):
-        member = lemma_col == token_row // lemma_tok + block * lemma_dev
-        live[block] = jnp.where(member & alive, 1.0, 0.0).astype(jnp.bfloat16)
+        first = -block * block_tok
+        member = (token_of >= first) & (token_of < lengths + first)
+        live[block] = jnp.where(member, 1.0, 0.0).astype(jnp.bfloat16)
 
     hid_copy.wait()
     in_float = hid[...].astype(jnp.float32)
     inv_rms = lax.rsqrt(jnp.mean(in_float * in_float, axis=1, keepdims=True) + norm_eps)
-    scaled = (in_float * inv_rms * gain_ref[...]).astype(jnp.bfloat16)
+    scaled = (in_float * inv_rms * gain_row).astype(jnp.bfloat16)
     scaled_b[...] = scaled
     scaled_t[...] = scaled.T
 
@@ -293,6 +296,8 @@
     tok_lse = token_temp * jnp.log(total)
     first_state = (me * group_axis + grp) * states_dev
     ratios = []
+    losses = jnp.zeros((1, 128), jnp.float32)
+    lane = lax.broadcasted_iota(jnp.int32, (1, 128), 1)
     for state in range(states_dev):
         length = qlen_ref[first_state + state]
         target = pos_ref[first_state + state]
@@ -307,9 +312,10 @@
         partition = jnp.sum(powers, axis=1, keepdims=True)
         pos_score = jnp.sum(similarity * is_positive, axis=1, keepdims=True)
         loss = jnp.log(partition) - pos_score / state_temp
-        loss_ref[state] = jnp.sum(loss)
+        losses = jnp.where(lane == state, loss, losses)
         grad_sim = loss_scale * (powers / partition - is_positive) / state_temp
         ratios.append(live_rows * (grad_sim / length_f) / total[span])
+    loss_ref[...] = losses
     ratio = jnp.concatenate(ratios, axis=0).astype(jnp.bfloat16)
 
     unit_grad = jnp.zeros((rows, proj_width), jnp.float32)
@@ -350,7 +356,7 @@
     )
     row_dot = jnp.sum(projected * proj_grad_b.astype(jnp.float32), axis=1, keepdims=True)
     hout[...] = (
-        inv_rms * (scaled_grad * gain_ref[...])
+        inv_rms * (scaled_grad * gain_row)
         - hid[...].astype(jnp.float32) * (inv_rms * inv_rms * row_dot / width)
     ).astype(jnp.bfloat16)
     hout_copy = pltpu.make_async_copy(hout, hgrad_ref, local_sem.at[3])
@@ -390,7 +396,7 @@
 
     weight_raw = raw[...].reshape(wrows, proj_width).astype(jnp.float32)
     ones = jnp.ones((8, proj_width), jnp.float32)
-    own_gain = gain_ref[:, pl.ds(pl.multiple_of(grp * wrows, 128), wrows)]
+    own_gain = gain_ref[pl.ds(pl.multiple_of(grp * wrows, 128), wrows)].reshape(1, wrows)
     gain_raw = lax.dot_general(
         ones, w_all[grp].astype(jnp.float32) * weight_raw, NT,
         preferred_element_type=jnp.float32, precision=lax.Precision.HIGHEST,
@@ -417,6 +423,19 @@
     for copy in w_out + k_out + wf_out + kf_out + a_out + s_out:
         copy.wait_send()
     hout_copy.wait()
+
+
+def place_kernel(loss, hgrad, wgrad, ggrad, loss_out, hgrad_out, wgrad_out, ggrad_out, sems):
+    copies = [
+        pltpu.make_async_copy(hgrad, hgrad_out, sems.at[0]),
+        pltpu.make_async_copy(wgrad, wgrad_out, sems.at[1]),
+    ]
+    for copy in copies:
+        copy.start()
+    loss_out[...] = loss[0, : loss_out.shape[0]]
+    ggrad_out[...] = ggrad[...].reshape(ggrad_out.shape)
+    for copy in copies:
+        copy.wait()
 
 
 def fused_body(hidden, gain, weight, lemma_emb, lemma_len, query_len, positive):
@@ -430,7 +449,7 @@
     lemmas_all = lemma_dev * lemma_axis
     vmem = pl.BlockSpec(memory_space=pltpu.VMEM)
     smem = pl.BlockSpec(memory_space=pltpu.SMEM)
-    hbm = pl.BlockSpec(memory_space=pl.ANY)
+    hbm = pl.BlockSpec(memory_space=pltpu.HBM)
     sem = pltpu.SemaphoreType.DMA
     bf16, f32 = jnp.bfloat16, jnp.float32
     outs = pl.pallas_call(
@@ -438,13 +457,13 @@
             fused_kernel, lemma_axis, group_axis, lemma_dev, lemma_tok, states_dev, query_tok
         ),
         out_shape=(
-            jax.ShapeDtypeStruct((states_dev,), f32),
+            jax.ShapeDtypeStruct((1, 128), f32),
             jax.ShapeDtypeStruct((rows, width), bf16),
             jax.ShapeDtypeStruct((wrows, proj_width), f32),
             jax.ShapeDtypeStruct((1, wrows), f32),
         ),
         in_specs=[hbm, vmem, hbm, hbm, vmem, smem, smem],
-        out_specs=(smem, hbm, vmem, vmem),
+        out_specs=(vmem, hbm, vmem, vmem),
         scratch_shapes=[
             pltpu.VMEM((rows, width), bf16),
             pltpu.VMEM((block_tok, proj_width), bf16),
@@ -473,7 +492,7 @@
             sem((group_axis,)), sem((group_axis,)),
         ],
         compiler_params=pltpu.CompilerParams(
-            collective_id=0, has_side_effects=True, vmem_limit_bytes=48 * 1024 * 1024
+            collective_id=0, has_side_effects=True, vmem_limit_bytes=62 * 1024 * 1024
         ),
         cost_estimate=pl.CostEstimate(
             flops=2 * rows * proj_width * (3 * width + 4 * block_tok * lemma_axis),
@@ -481,12 +500,24 @@
             transcendentals=rows * block_tok * lemma_axis,
         ),
     )(
-        hidden.reshape(rows, width), gain.reshape(1, width), weight,
-        lemma_emb.reshape(block_tok, proj_width), lemma_len.reshape(1, lemmas_all),
+        hidden.reshape(rows, width), gain, weight,
+        lemma_emb.reshape(block_tok, proj_width), lemma_len,
         query_len, positive,
     )
-    loss, hidden_grad, weight_grad, gain_grad = outs
-    return (loss, hidden_grad.reshape(hidden.shape), weight_grad, gain_grad.reshape(wrows))
+    loss, hidden_grad, weight_grad, gain_grad = pl.pallas_call(
+        place_kernel,
+        out_shape=(
+            jax.ShapeDtypeStruct((states_dev,), f32),
+            jax.ShapeDtypeStruct((rows, width), bf16),
+            jax.ShapeDtypeStruct((wrows, proj_width), f32),
+            jax.ShapeDtypeStruct((wrows,), f32),
+        ),
+        in_specs=[vmem, pl.BlockSpec(memory_space=pl.ANY), pl.BlockSpec(memory_space=pl.ANY), vmem],
+        out_specs=(vmem, hbm, hbm, vmem),
+        scratch_shapes=[sem((2,))],
+        compiler_params=pltpu.CompilerParams(vmem_limit_bytes=62 * 1024 * 1024),
+    )(*outs)
+    return (loss, hidden_grad.reshape(hidden.shape), weight_grad, gain_grad)
 
 
 def solution(mesh):

time: 43.6 us -> 57.6 us (1.32)
  Pallas kernels: 36.7 us -> 56.8 us
  local copies, waits for them, and re-layouts: 5.45 us -> 0 us
  other arithmetic: 0.6 us -> 0 us
    pallas_call x0 -> x1, Pallas kernels: none -> 20.2 us  [fused_body(): pl.pallas_call(place_kernel, out_shape=(jax.ShapeDtypeStruct((states_dev,...]
    unnamed x15 -> x0, local copies, waits for them, and re-layouts: 4.73 us -> none
    reshape x1 -> x0, local copies, waits for them, and re-layouts: 0.72 us -> none  [fused_body(): gain.reshape(1, width)]
    pallas_call x1 -> x0, other arithmetic: 0.6 us -> none  [fused_body(): pl.pallas_call(functools.partial(fused_kernel, lemma_axis, group_axis, le...]
where the time goes in v2:
time: 57.6 us; the launch traced here: 57.4 us
  Pallas kernels  56.8 us (99%)
  between operations  0.64 us (1%)
    pallas_call x1, Pallas kernels, fused_body(): pl.pallas_call(functools.partial(fused_kernel, lemma_axis, group_axis, le...  36.5 us
    pallas_call x1, Pallas kernels, fused_body(): pl.pallas_call(place_kernel, out_shape=(jax.ShapeDtypeStruct((states_dev,...  20.2 us

profile of v2, /device:TPU:0, one launch (start us, length us, event | category | flops | bytes accessed | tf_op | source)
XLA Modules:
  0.0 57.4 jit_solution(601399636180122431)
XLA Ops:
  0.6 36.5 %shard_map.102 = (f32[1,128]{1,0:T(1,128)}, bf16[128,1536]{1,0:T(8,128)(2,1)}, f32[384,128]{1,0:T(8,128)}, f32[1,384]{1,0:T(1,128)}) custom-call(bf16[128,1536]{1,0:T(8,128)(2,1)} %bitcast.3, f32[1536]{0:T(1024)} %gain_ref.1, bf16[384,128]{1,0:T(8,128)(2,1)} %weight_ref.1, bf16[512,128]{1,0:T(8,128)(2,1)} %bitcast.5, s32[128]{0:T(128)} %len_ref.1, ...), custom_call_target="tpu_custom_call" | custom-call | flops 687865856 | bytes 1572864 | tf_op jit(solution)/shard_map/pallas_call | solution.py:455
  37.2 20.2 %shard_map.103 = (f32[2]{0:T(128)}, bf16[128,1536]{1,0:T(8,128)(2,1)}, f32[384,128]{1,0:T(8,128)}, f32[384]{0:T(512)}) custom-call(f32[1,128]{1,0:T(1,128)} %get-tuple-element.12.loss, bf16[128,1536]{1,0:T(8,128)(2,1)} %get-tuple-element.13.hgrad, f32[384,128]{1,0:T(8,128)} %get-tuple-element.14.wgrad, f32[1,384]{1,0:T(1,128)} %get-tuple-element.15.ggrad), custom_call_target="tpu_custom_call" | custom-call | tf_op jit(solution)/shard_map/pallas_call | solution.py:507

commit v3 on v2

--- a/solution.py
+++ b/solution.py
@@ -160,9 +160,9 @@
     hidden_ref, gain_ref, weight_ref, emb_ref, len_ref, qlen_ref, pos_ref,
     loss_ref, hgrad_ref, wgrad_ref, ggrad_ref,
     hid, emb, hout, w_all, keys, live, powers_b, scaled_b, scaled_t,
-    part, pair_in, half, chip_in, quarter, grp_in, raw, sq,
+    part, pair_in, half, chip_in, quarter, grp_in, raw, sq, over_gain,
     local_sem, w_send, w_recv, wf_send, wf_recv, k_send, k_recv, kf_send, kf_recv,
-    p_sem, c_send, c_recv, g_send, g_recv, a_send, a_recv, s_send, s_recv,
+    p_send, p_recv, c_send, c_recv, g_send, g_recv, a_send, a_recv, s_send, s_recv,
 ):
     chips = lemma_axis // 2
     me, grp = lax.axis_index("lemma"), lax.axis_index("grp")
@@ -176,11 +176,25 @@
     block_tok = lemma_dev * lemma_tok
     lemmas_all = lemma_dev * lemma_axis
 
+    across = 2 - chips % 2
+    along = chips // across
+    chip_y, chip_x = chip // across, lax.rem(chip, across)
+
+    def chip_to(step):
+        step_y, step_x = step // across, step % across
+        return lax.rem(chip_y + step_y, along) * across + lax.rem(chip_x + step_x, across)
+
+    def chip_source(step):
+        step_y, step_x = step // across, step % across
+        return lax.rem(chip_y + along - step_y, along) * across + lax.rem(
+            chip_x + across - step_x, across
+        )
+
     def chip_peer(step):
-        return lax.rem(chip + step, chips) * 2 + core
+        return chip_to(step) * 2 + core
 
     def chip_from(step):
-        return lax.rem(chip + chips - step, chips) * 2 + core
+        return chip_source(step) * 2 + core
 
     def grp_peer(step):
         return lax.rem(grp + step, group_axis)
@@ -202,12 +216,17 @@
     hid_copy.start()
 
     barrier = pltpu.get_barrier_semaphore()
-    for step in range(1, lemma_axis):
+    others = [
+        (lemma_step, grp_step)
+        for lemma_step in range(lemma_axis)
+        for grp_step in range(group_axis)
+        if lemma_step or grp_step
+    ]
+    for lemma_step, grp_step in others:
         pl.semaphore_signal(
-            barrier, inc=1, device_id=(lax.rem(me + step, lemma_axis), grp), device_id_type=MESH
-        )
-    for step in range(1, group_axis):
-        pl.semaphore_signal(barrier, inc=1, device_id=(me, grp_peer(step)), device_id_type=MESH)
+            barrier, inc=1, device_id_type=MESH,
+            device_id=(lax.rem(me + lemma_step, lemma_axis), grp_peer(grp_step)),
+        )
 
     emb_copy.wait()
     tokens = emb[...].astype(jnp.float32)
@@ -216,7 +235,7 @@
     ) / math.sqrt(proj_width)
     keys[me] = (tokens * token_scale).astype(jnp.bfloat16)
     w_copy.wait()
-    pl.semaphore_wait(barrier, lemma_axis - 1 + group_axis - 1)
+    pl.semaphore_wait(barrier, len(others))
 
     my_half = pl.ds(pl.multiple_of(core * hrows, hrows), hrows)
     w_out = []
@@ -226,7 +245,7 @@
         copy.start()
         w_out.append(copy)
     k_out = []
-    for step in range(1, chips):
+    for step in reversed(range(1, chips)):
         copy = remote(
             keys.at[me], keys.at[me], k_send.at[step], k_recv.at[step], chip_peer(step), grp
         )
@@ -251,6 +270,10 @@
     scaled_b[...] = scaled
     scaled_t[...] = scaled.T
 
+    own_gain = gain_ref[pl.ds(pl.multiple_of(grp * wrows, 128), wrows)].reshape(1, wrows)
+    gain_col = jnp.broadcast_to(own_gain, (proj_width, wrows)).T
+    over_gain[...] = (w_all[grp].astype(jnp.float32) / gain_col).reshape(over_gain.shape)
+
     wf_out = []
     for step in range(1, group_axis):
         dst = w_all.at[grp_from(step), my_half]
@@ -258,12 +281,6 @@
         copy = remote(dst, dst, wf_send.at[step], wf_recv.at[step], pair, grp)
         copy.start()
         wf_out.append(copy)
-    for step in range(1, chips):
-        dst = keys.at[chip_from(step)]
-        remote(dst, dst, k_send.at[step], k_recv.at[step], chip_peer(step), grp).wait_recv()
-        copy = remote(dst, dst, kf_send.at[step], kf_recv.at[step], pair, grp)
-        copy.start()
-        kf_out.append(copy)
     other_half = pl.ds(pl.multiple_of((1 - core) * hrows, hrows), hrows)
     for step in range(1, group_axis):
         dst = w_all.at[grp_from(step), other_half]
@@ -284,14 +301,24 @@
         powers_b[block] = exp_terms
         return total + jnp.dot(exp_terms, live[block], preferred_element_type=jnp.float32)
 
+    def from_pair(step):
+        block = chip_source(step) * 2 + (1 - core)
+        dst = keys.at[block]
+        remote(dst, dst, kf_send.at[step], kf_recv.at[step], pair, grp).wait_recv()
+        return block
+
     total = first_pass(me, jnp.zeros((rows, lemmas_all), jnp.float32))
+    total = first_pass(from_pair(0), total)
+    for step in range(1, chips):
+        dst = keys.at[chip_from(step)]
+        remote(dst, dst, k_send.at[step], k_recv.at[step], chip_peer(step), grp).wait_recv()
+        copy = remote(dst, dst, kf_send.at[step], kf_recv.at[step], pair, grp)
+        copy.start()
+        kf_out.append(copy)
     for step in range(1, chips):
         total = first_pass(chip_from(step), total)
-    for step in range(chips):
-        block = lax.rem(chip + chips - step, chips) * 2 + (1 - core)
-        dst = keys.at[block]
-        remote(dst, dst, kf_send.at[step], kf_recv.at[step], pair, grp).wait_recv()
-        total = first_pass(block, total)
+    for step in range(1, chips):
+        total = first_pass(from_pair(step), total)
 
     tok_lse = token_temp * jnp.log(total)
     first_state = (me * group_axis + grp) * states_dev
@@ -336,20 +363,29 @@
             part[owner % 2, owner // 2, group] = weight_part[start : start + piece].astype(
                 jnp.bfloat16
             )
-    pair_copy = remote(part.at[1 - core], pair_in, p_sem.at[0], p_sem.at[1], pair, grp)
-    pair_copy.start()
-    pair_copy.wait()
-    half[...] = (part[core].astype(jnp.float32) + pair_in[...].astype(jnp.float32)).astype(
-        jnp.bfloat16
-    )
+    order = list(reversed(range(chips)))
+    p_out = []
+    for step in order:
+        target = chip_to(step)
+        copy = remote(
+            part.at[1 - core, target], pair_in.at[step], p_send.at[step], p_recv.at[step], pair, grp
+        )
+        copy.start()
+        p_out.append(copy)
     c_out = []
-    for step in range(1, chips):
-        copy = remote(
-            half.at[lax.rem(chip + step, chips)], chip_in.at[step - 1],
-            c_send.at[step], c_recv.at[step], chip_peer(step), grp,
-        )
-        copy.start()
-        c_out.append(copy)
+    for step, pair_copy in zip(order, p_out):
+        target = chip_to(step)
+        pair_copy.wait_recv()
+        half[step] = (
+            part[core, target].astype(jnp.float32) + pair_in[step].astype(jnp.float32)
+        ).astype(jnp.bfloat16)
+        if step:
+            copy = remote(
+                half.at[step], chip_in.at[step - 1],
+                c_send.at[step], c_recv.at[step], chip_peer(step), grp,
+            )
+            copy.start()
+            c_out.append(copy)
 
     scaled_grad = lax.dot_general(
         proj_grad_b, w_all[...].reshape(width, proj_width), NT, preferred_element_type=jnp.float32
@@ -364,7 +400,7 @@
 
     for copy in c_out:
         copy.wait()
-    chip_sum = half[chip].astype(jnp.float32)
+    chip_sum = half[0].astype(jnp.float32)
     for step in range(1, chips):
         chip_sum += chip_in[step - 1].astype(jnp.float32)
     quarter[...] = chip_sum.astype(jnp.bfloat16)
@@ -381,7 +417,8 @@
     grp_sum = quarter[grp].astype(jnp.float32)
     for step in range(1, group_axis):
         grp_sum += grp_in[step - 1].astype(jnp.float32)
-    raw[me] = grp_sum.astype(jnp.bfloat16)
+    own_raw = grp_sum.astype(jnp.bfloat16)
+    raw[me] = own_raw
     a_out = []
     for step in range(1, lemma_axis):
         copy = remote(
@@ -390,51 +427,60 @@
         )
         copy.start()
         a_out.append(copy)
+    own_raw = own_raw.astype(jnp.float32)
+    own_gain_raw = jnp.sum(own_raw * over_gain[me], axis=1, keepdims=True)
+    squares = jnp.sum(own_raw * own_raw) + jnp.sum(own_gain_raw * own_gain_raw)
+    my_sq = sq.at[grp * lemma_axis + me]
+    my_sq[...] = jnp.full((1, 128), squares, jnp.float32)
+    for lemma_step, grp_step in others:
+        copy = remote(
+            my_sq, my_sq, s_send, s_recv,
+            lax.rem(me + lemma_step, lemma_axis), grp_peer(grp_step),
+        )
+        copy.start()
     for step in range(1, lemma_axis):
         dst = raw.at[lax.rem(me + lemma_axis - step, lemma_axis)]
-        remote(dst, dst, a_send.at[step], a_recv.at[step], me, grp_peer(1)).wait_recv()
+        remote(dst, dst, a_send.at[step], a_recv.at[step], pair, grp).wait_recv()
 
     weight_raw = raw[...].reshape(wrows, proj_width).astype(jnp.float32)
     ones = jnp.ones((8, proj_width), jnp.float32)
-    own_gain = gain_ref[pl.ds(pl.multiple_of(grp * wrows, 128), wrows)].reshape(1, wrows)
     gain_raw = lax.dot_general(
-        ones, w_all[grp].astype(jnp.float32) * weight_raw, NT,
+        ones, over_gain[...].reshape(wrows, proj_width) * weight_raw, NT,
         preferred_element_type=jnp.float32, precision=lax.Precision.HIGHEST,
-    )[:1] / own_gain
-    squares = jnp.sum(weight_raw * weight_raw) + jnp.sum(gain_raw * gain_raw)
-    sq[grp] = jnp.full((8, 128), squares, jnp.float32)
-    s_out = []
-    for step in range(1, group_axis):
-        copy = remote(
-            sq.at[grp], sq.at[grp], s_send.at[step], s_recv.at[step], me, grp_peer(step)
-        )
-        copy.start()
-        s_out.append(copy)
-    for step in range(1, group_axis):
-        dst = sq.at[grp_from(step)]
-        remote(dst, dst, s_send.at[step], s_recv.at[step], me, grp_peer(step)).wait_recv()
-    squares_all = sq[0, :1, :]
-    for group in range(1, group_axis):
-        squares_all += sq[group, :1, :]
+    )[:1]
+    all_but_one = sq.at[pl.ds(0, len(others))]
+    remote(all_but_one, all_but_one, s_send, s_recv, pair, grp).wait()
+    squares_all = jnp.sum(sq[...], axis=0)
     factor = jnp.minimum(1.0, grad_limit / jnp.sqrt(squares_all + norm_eps))
     wgrad_ref[...] = weight_raw * factor
     ggrad_ref[...] = gain_raw * factor[:, :1]
 
-    for copy in w_out + k_out + wf_out + kf_out + a_out + s_out:
+    for copy in w_out + k_out + wf_out + kf_out + p_out + a_out:
         copy.wait_send()
     hout_copy.wait()
 
 
-def place_kernel(loss, hgrad, wgrad, ggrad, loss_out, hgrad_out, wgrad_out, ggrad_out, sems):
-    copies = [
-        pltpu.make_async_copy(hgrad, hgrad_out, sems.at[0]),
-        pltpu.make_async_copy(wgrad, wgrad_out, sems.at[1]),
-    ]
+def place_kernel(
+    loss, hgrad, wgrad, ggrad, loss_out, hgrad_out, wgrad_out, ggrad_out,
+    loss_in, hbuf, wbuf, ggrad_in, loss_row, ggrad_row, sems,
+):
+    pairs = [(hgrad, hbuf), (wgrad, wbuf), (loss, loss_in), (ggrad, ggrad_in)]
+    copies = [pltpu.make_async_copy(a, b, sems.at[i]) for i, (a, b) in enumerate(pairs)]
     for copy in copies:
         copy.start()
-    loss_out[...] = loss[0, : loss_out.shape[0]]
-    ggrad_out[...] = ggrad[...].reshape(ggrad_out.shape)
-    for copy in copies:
+    pairs = [(hbuf, hgrad_out), (wbuf, wgrad_out), (loss_row, loss_out), (ggrad_row, ggrad_out)]
+    backs = [pltpu.make_async_copy(a, b, sems.at[4 + i]) for i, (a, b) in enumerate(pairs)]
+    copies[0].wait()
+    backs[0].start()
+    copies[1].wait()
+    backs[1].start()
+    copies[2].wait()
+    loss_row[...] = loss_in[0, : loss_row.shape[0]]
+    backs[2].start()
+    copies[3].wait()
+    ggrad_row[...] = ggrad_in[...].reshape(ggrad_row.shape)
+    backs[3].start()
+    for copy in backs:
         copy.wait()
 
 
@@ -481,15 +527,16 @@
             pltpu.VMEM((group_axis, piece, proj_width), bf16),
             pltpu.VMEM((group_axis - 1, piece, proj_width), bf16),
             pltpu.VMEM((lemma_axis, piece, proj_width), bf16),
-            pltpu.VMEM((group_axis, 8, 128), f32),
+            pltpu.VMEM((group_axis * lemma_axis, 1, 128), f32),
+            pltpu.VMEM((lemma_axis, piece, proj_width), f32),
             sem((4,)),
             sem((group_axis,)), sem((group_axis,)), sem((group_axis,)), sem((group_axis,)),
             sem((chips,)), sem((chips,)), sem((chips,)), sem((chips,)),
-            sem((2,)),
+            sem((chips,)), sem((chips,)),
             sem((chips,)), sem((chips,)),
             sem((group_axis,)), sem((group_axis,)),
             sem((lemma_axis,)), sem((lemma_axis,)),
-            sem((group_axis,)), sem((group_axis,)),
+            sem, sem,
         ],
         compiler_params=pltpu.CompilerParams(
             collective_id=0, has_side_effects=True, vmem_limit_bytes=62 * 1024 * 1024
@@ -512,9 +559,17 @@
             jax.ShapeDtypeStruct((wrows, proj_width), f32),
             jax.ShapeDtypeStruct((wrows,), f32),
         ),
-        in_specs=[vmem, pl.BlockSpec(memory_space=pl.ANY), pl.BlockSpec(memory_space=pl.ANY), vmem],
-        out_specs=(vmem, hbm, hbm, vmem),
-        scratch_shapes=[sem((2,))],
+        in_specs=[hbm] * 4,
+        out_specs=(hbm,) * 4,
+        scratch_shapes=[
+            pltpu.VMEM((1, 128), f32),
+            pltpu.VMEM((rows, width), bf16),
+            pltpu.VMEM((wrows, proj_width), f32),
+            pltpu.VMEM((1, wrows), f32),
+            pltpu.VMEM((states_dev,), f32),
+            pltpu.VMEM((wrows,), f32),
+            sem((8,)),
+        ],
         compiler_params=pltpu.CompilerParams(vmem_limit_bytes=62 * 1024 * 1024),
     )(*outs)
     return (loss, hidden_grad.reshape(hidden.shape), weight_grad, gain_grad)

time: 57.6 us -> 37.2 us (0.65)
  Pallas kernels: 56.8 us -> 36.3 us
    pallas_call x1, Pallas kernels: 20.2 us -> 1.88 us  [fused_body(): pl.pallas_call(place_kernel, out_shape=(jax.ShapeDtypeStruct((states_dev,...]
    pallas_call x1, Pallas kernels: 36.5 us -> 34.5 us  [fused_body(): pl.pallas_call(functools.partial(fused_kernel, lemma_axis, group_axis, le...]
where the time goes in v3:
time: 37.2 us; the launch traced here: 37 us
  Pallas kernels  36.3 us (98%)
  between operations  0.64 us (2%)
    pallas_call x1, Pallas kernels, fused_body(): pl.pallas_call(functools.partial(fused_kernel, lemma_axis, group_axis, le...  34.5 us
    pallas_call x1, Pallas kernels, fused_body(): pl.pallas_call(place_kernel, out_shape=(jax.ShapeDtypeStruct((states_dev,...  1.88 us

profile of v3, /device:TPU:0, one launch (start us, length us, event | category | flops | bytes accessed | tf_op | source)
XLA Modules:
  0.0 37.0 jit_solution(4538565698208120848)
XLA Ops:
  0.6 34.5 %shard_map.102 = (f32[1,128]{1,0:T(1,128)}, bf16[128,1536]{1,0:T(8,128)(2,1)}, f32[384,128]{1,0:T(8,128)}, f32[1,384]{1,0:T(1,128)}) custom-call(bf16[128,1536]{1,0:T(8,128)(2,1)} %bitcast.3, f32[1536]{0:T(1024)} %gain_ref.1, bf16[384,128]{1,0:T(8,128)(2,1)} %weight_ref.1, bf16[512,128]{1,0:T(8,128)(2,1)} %bitcast.5, s32[128]{0:T(128)} %len_ref.1, ...), custom_call_target="tpu_custom_call" | custom-call | flops 687865856 | bytes 1572864 | tf_op jit(solution)/shard_map/pallas_call | solution.py:501
  35.1 1.9 %shard_map.103 = (f32[2]{0:T(128)}, bf16[128,1536]{1,0:T(8,128)(2,1)}, f32[384,128]{1,0:T(8,128)}, f32[384]{0:T(512)}) custom-call(f32[1,128]{1,0:T(1,128)} %get-tuple-element.12.loss, bf16[128,1536]{1,0:T(8,128)(2,1)} %get-tuple-element.13.hgrad, f32[384,128]{1,0:T(8,128)} %get-tuple-element.14.wgrad, f32[1,384]{1,0:T(1,128)} %get-tuple-element.15.ggrad), custom_call_target="tpu_custom_call" | custom-call | tf_op jit(solution)/shard_map/pallas_call | solution.py:554

commit v4 on v3

--- a/solution.py
+++ b/solution.py
@@ -159,7 +159,7 @@
     lemma_axis, group_axis, lemma_dev, lemma_tok, states_dev, query_tok,
     hidden_ref, gain_ref, weight_ref, emb_ref, len_ref, qlen_ref, pos_ref,
     loss_ref, hgrad_ref, wgrad_ref, ggrad_ref,
-    hid, emb, hout, w_all, keys, live, powers_b, scaled_b, scaled_t,
+    hid, emb, hout, w_all, keys, live, live_t, powers_b, scaled_b, scaled_t,
     part, pair_in, half, chip_in, quarter, grp_in, raw, sq, over_gain,
     local_sem, w_send, w_recv, wf_send, wf_recv, k_send, k_recv, kf_send, kf_recv,
     p_send, p_recv, c_send, c_recv, g_send, g_recv, a_send, a_recv, s_send, s_recv,
@@ -233,7 +233,7 @@
     token_scale = lax.rsqrt(
         jnp.mean(tokens * tokens, axis=1, keepdims=True) + norm_eps
     ) / math.sqrt(proj_width)
-    keys[me] = (tokens * token_scale).astype(jnp.bfloat16)
+    keys[chip, core] = (tokens * token_scale).astype(jnp.bfloat16)
     w_copy.wait()
     pl.semaphore_wait(barrier, len(others))
 
@@ -247,28 +247,42 @@
     k_out = []
     for step in reversed(range(1, chips)):
         copy = remote(
-            keys.at[me], keys.at[me], k_send.at[step], k_recv.at[step], chip_peer(step), grp
+            keys.at[chip, core], keys.at[chip, core], k_send.at[step], k_recv.at[step], chip_peer(step), grp
         )
         copy.start()
         k_out.append(copy)
-    kf_out = [remote(keys.at[me], keys.at[me], kf_send.at[0], kf_recv.at[0], pair, grp)]
+    kf_out = [remote(keys.at[chip, core], keys.at[chip, core], kf_send.at[0], kf_recv.at[0], pair, grp)]
     kf_out[0].start()
 
+    chip_tok = 2 * block_tok
     token_of = lax.broadcasted_iota(
-        jnp.int32, (block_tok, lemmas_all), 0
-    ) - lemma_tok * lax.broadcasted_iota(jnp.int32, (block_tok, lemmas_all), 1)
+        jnp.int32, (chip_tok, lemmas_all), 0
+    ) - lemma_tok * lax.broadcasted_iota(jnp.int32, (chip_tok, lemmas_all), 1)
+    token_of_t = lax.broadcasted_iota(
+        jnp.int32, (lemmas_all, chip_tok), 1
+    ) - lemma_tok * lax.broadcasted_iota(jnp.int32, (lemmas_all, chip_tok), 0)
     lengths = jnp.minimum(len_ref[...].reshape(1, lemmas_all), lemma_tok)
-    for block in range(lemma_axis):
-        first = -block * block_tok
+    lengths_t = jnp.broadcast_to(
+        lengths.astype(jnp.float32), (lemmas_all, lemmas_all)
+    ).T[:, :1].astype(jnp.int32)
+    for block in range(chips):
+        first = -block * chip_tok
         member = (token_of >= first) & (token_of < lengths + first)
         live[block] = jnp.where(member, 1.0, 0.0).astype(jnp.bfloat16)
+        member = (token_of_t >= first) & (token_of_t < lengths_t + first)
+        live_t[block] = jnp.where(member, 1.0, 0.0).astype(jnp.bfloat16)
 
     hid_copy.wait()
     in_float = hid[...].astype(jnp.float32)
     inv_rms = lax.rsqrt(jnp.mean(in_float * in_float, axis=1, keepdims=True) + norm_eps)
     scaled = (in_float * inv_rms * gain_row).astype(jnp.bfloat16)
     scaled_b[...] = scaled
-    scaled_t[...] = scaled.T
+    scaled_rows = scaled.T
+    piece = wrows // lemma_axis
+    for group in range(group_axis):
+        for owner in range(lemma_axis):
+            start = group * wrows + owner * piece
+            scaled_t[owner // 2, owner % 2, group] = scaled_rows[start : start + piece]
 
     own_gain = gain_ref[pl.ds(pl.multiple_of(grp * wrows, 128), wrows)].reshape(1, wrows)
     gain_col = jnp.broadcast_to(own_gain, (proj_width, wrows)).T
@@ -295,30 +309,31 @@
 
     def first_pass(block, total):
         scores = lax.dot_general(
-            query_unit, keys[block], NT, preferred_element_type=jnp.float32
+            query_unit, keys[block].reshape(chip_tok, proj_width), NT, preferred_element_type=jnp.float32
         )
         exp_terms = jnp.exp(scores * (1.0 / token_temp)).astype(jnp.bfloat16)
         powers_b[block] = exp_terms
         return total + jnp.dot(exp_terms, live[block], preferred_element_type=jnp.float32)
 
-    def from_pair(step):
-        block = chip_source(step) * 2 + (1 - core)
-        dst = keys.at[block]
-        remote(dst, dst, kf_send.at[step], kf_recv.at[step], pair, grp).wait_recv()
-        return block
-
-    total = first_pass(me, jnp.zeros((rows, lemmas_all), jnp.float32))
-    total = first_pass(from_pair(0), total)
-    for step in range(1, chips):
-        dst = keys.at[chip_from(step)]
+    def forward(step):
+        dst = keys.at[chip_source(step), core]
         remote(dst, dst, k_send.at[step], k_recv.at[step], chip_peer(step), grp).wait_recv()
         copy = remote(dst, dst, kf_send.at[step], kf_recv.at[step], pair, grp)
         copy.start()
         kf_out.append(copy)
+
+    def chip_pass(step, total):
+        source = chip_source(step)
+        dst = keys.at[source, 1 - core]
+        remote(dst, dst, kf_send.at[step], kf_recv.at[step], pair, grp).wait_recv()
+        return first_pass(source, total)
+
+    total = chip_pass(0, jnp.zeros((rows, lemmas_all), jnp.float32))
     for step in range(1, chips):
-        total = first_pass(chip_from(step), total)
-    for step in range(1, chips):
-        total = first_pass(from_pair(step), total)
+        forward(step)
+        if step > 1:
+            total = chip_pass(step - 1, total)
+    total = chip_pass(chips - 1, total)
 
     tok_lse = token_temp * jnp.log(total)
     first_state = (me * group_axis + grp) * states_dev
@@ -346,75 +361,84 @@
     ratio = jnp.concatenate(ratios, axis=0).astype(jnp.bfloat16)
 
     unit_grad = jnp.zeros((rows, proj_width), jnp.float32)
-    for block in range(lemma_axis):
-        spread = lax.dot_general(ratio, live[block], NT, preferred_element_type=jnp.float32)
+    for block in range(chips):
+        spread = jnp.dot(ratio, live_t[block], preferred_element_type=jnp.float32)
         coef = (powers_b[block].astype(jnp.float32) * spread).astype(jnp.bfloat16)
-        unit_grad += jnp.dot(coef, keys[block], preferred_element_type=jnp.float32)
+        unit_grad += jnp.dot(
+            coef, keys[block].reshape(chip_tok, proj_width), preferred_element_type=jnp.float32
+        )
     proj_grad = proj_scale * unit_grad - projected * (
         proj_scale * proj_scale * proj_scale
     ) * jnp.sum(projected * unit_grad, axis=1, keepdims=True)
     proj_grad_b = proj_grad.astype(jnp.bfloat16)
 
-    weight_part = jnp.dot(scaled_t[...], proj_grad_b, preferred_element_type=jnp.float32)
-    piece = wrows // lemma_axis
-    for group in range(group_axis):
-        for owner in range(lemma_axis):
-            start = group * wrows + owner * piece
-            part[owner % 2, owner // 2, group] = weight_part[start : start + piece].astype(
-                jnp.bfloat16
-            )
+    def weight_part(target, side):
+        left = scaled_t[target, side].reshape(group_axis * piece, rows)
+        return jnp.dot(left, proj_grad_b, preferred_element_type=jnp.float32).reshape(
+            group_axis, piece, proj_width
+        )
+
     order = list(reversed(range(chips)))
     p_out = []
     for step in order:
-        target = chip_to(step)
-        copy = remote(
-            part.at[1 - core, target], pair_in.at[step], p_send.at[step], p_recv.at[step], pair, grp
-        )
+        part[step] = weight_part(chip_to(step), 1 - core).astype(jnp.bfloat16)
+        copy = remote(part.at[step], pair_in.at[step], p_send.at[step], p_recv.at[step], pair, grp)
         copy.start()
         p_out.append(copy)
-    c_out = []
+    grp_order = list(reversed(range(group_axis)))
+    c_out = {}
     for step, pair_copy in zip(order, p_out):
-        target = chip_to(step)
+        mine = weight_part(chip_to(step), core)
         pair_copy.wait_recv()
-        half[step] = (
-            part[core, target].astype(jnp.float32) + pair_in[step].astype(jnp.float32)
+        half[step] = (mine + pair_in[step].astype(jnp.float32)).astype(jnp.bfloat16)
+        if step:
+            for grp_step in grp_order:
+                copy = remote(
+                    half.at[step, grp_peer(grp_step)], chip_in.at[step - 1, grp_step],
+                    c_send.at[step - 1, grp_step], c_recv.at[step - 1, grp_step],
+                    chip_peer(step), grp,
+                )
+                copy.start()
+                c_out[step, grp_step] = copy
+
+    row_dot = jnp.sum(projected * proj_grad_b.astype(jnp.float32), axis=1, keepdims=True)
+    row_scale = inv_rms * inv_rms * row_dot / width
+
+    def hidden_part(state):
+        span = slice(state * query_tok, (state + 1) * query_tok)
+        scaled_grad = lax.dot_general(
+            proj_grad_b[span], w_all[...].reshape(width, proj_width), NT,
+            preferred_element_type=jnp.float32,
+        )
+        hout[span] = (
+            inv_rms[span] * (scaled_grad * gain_row)
+            - hid[span].astype(jnp.float32) * row_scale[span]
         ).astype(jnp.bfloat16)
-        if step:
+        copy = pltpu.make_async_copy(hout.at[span], hgrad_ref.at[span], local_sem.at[3 + state])
+        copy.start()
+        return copy
+
+    hout_copies = [hidden_part(0)]
+
+    g_out = []
+    for grp_step in grp_order:
+        chip_sum = half[0, grp_peer(grp_step)].astype(jnp.float32)
+        for step in range(1, chips):
+            c_out[step, grp_step].wait_recv()
+            chip_sum += chip_in[step - 1, grp_step].astype(jnp.float32)
+        if grp_step:
+            quarter[grp_step] = chip_sum.astype(jnp.bfloat16)
             copy = remote(
-                half.at[step], chip_in.at[step - 1],
-                c_send.at[step], c_recv.at[step], chip_peer(step), grp,
+                quarter.at[grp_step], grp_in.at[grp_step - 1],
+                g_send.at[grp_step], g_recv.at[grp_step], me, grp_peer(grp_step),
             )
             copy.start()
-            c_out.append(copy)
-
-    scaled_grad = lax.dot_general(
-        proj_grad_b, w_all[...].reshape(width, proj_width), NT, preferred_element_type=jnp.float32
-    )
-    row_dot = jnp.sum(projected * proj_grad_b.astype(jnp.float32), axis=1, keepdims=True)
-    hout[...] = (
-        inv_rms * (scaled_grad * gain_row)
-        - hid[...].astype(jnp.float32) * (inv_rms * inv_rms * row_dot / width)
-    ).astype(jnp.bfloat16)
-    hout_copy = pltpu.make_async_copy(hout, hgrad_ref, local_sem.at[3])
-    hout_copy.start()
-
-    for copy in c_out:
-        copy.wait()
-    chip_sum = half[0].astype(jnp.float32)
-    for step in range(1, chips):
-        chip_sum += chip_in[step - 1].astype(jnp.float32)
-    quarter[...] = chip_sum.astype(jnp.bfloat16)
-    g_out = []
-    for step in range(1, group_axis):
-        copy = remote(
-            quarter.at[grp_peer(step)], grp_in.at[step - 1],
-            g_send.at[step], g_recv.at[step], me, grp_peer(step),
-        )
-        copy.start()
-        g_out.append(copy)
+            g_out.append(copy)
+        else:
+            grp_sum = chip_sum
+    hout_copies += [hidden_part(state) for state in range(1, states_dev)]
     for copy in g_out:
-        copy.wait()
-    grp_sum = quarter[grp].astype(jnp.float32)
+        copy.wait_recv()
     for step in range(1, group_axis):
         grp_sum += grp_in[step - 1].astype(jnp.float32)
     own_raw = grp_sum.astype(jnp.bfloat16)
@@ -455,9 +479,10 @@
     wgrad_ref[...] = weight_raw * factor
     ggrad_ref[...] = gain_raw * factor[:, :1]
 
-    for copy in w_out + k_out + wf_out + kf_out + p_out + a_out:
+    for copy in w_out + k_out + wf_out + kf_out + p_out + list(c_out.values()) + g_out + a_out:
         copy.wait_send()
-    hout_copy.wait()
+    for copy in hout_copies:
+        copy.wait()
 
 
 def place_kernel(
@@ -515,12 +540,13 @@
             pltpu.VMEM((block_tok, proj_width), bf16),
             pltpu.VMEM((rows, width), bf16),
             pltpu.VMEM((group_axis, wrows, proj_width), bf16),
-            pltpu.VMEM((lemma_axis, block_tok, proj_width), bf16),
-            pltpu.VMEM((lemma_axis, block_tok, lemmas_all), bf16),
-            pltpu.VMEM((lemma_axis, rows, block_tok), bf16),
+            pltpu.VMEM((chips, 2, block_tok, proj_width), bf16),
+            pltpu.VMEM((chips, 2 * block_tok, lemmas_all), bf16),
+            pltpu.VMEM((chips, lemmas_all, 2 * block_tok), bf16),
+            pltpu.VMEM((chips, rows, 2 * block_tok), bf16),
             pltpu.VMEM((rows, width), bf16),
-            pltpu.VMEM((width, rows), bf16),
-            pltpu.VMEM((2, chips, group_axis, piece, proj_width), bf16),
+            pltpu.VMEM((chips, 2, group_axis, piece, rows), bf16),
+            pltpu.VMEM((chips, group_axis, piece, proj_width), bf16),
             pltpu.VMEM((chips, group_axis, piece, proj_width), bf16),
             pltpu.VMEM((chips, group_axis, piece, proj_width), bf16),
             pltpu.VMEM((chips - 1, group_axis, piece, proj_width), bf16),
@@ -529,11 +555,11 @@
             pltpu.VMEM((lemma_axis, piece, proj_width), bf16),
             pltpu.VMEM((group_axis * lemma_axis, 1, 128), f32),
             pltpu.VMEM((lemma_axis, piece, proj_width), f32),
-            sem((4,)),
+            sem((3 + states_dev,)),
             sem((group_axis,)), sem((group_axis,)), sem((group_axis,)), sem((group_axis,)),
             sem((chips,)), sem((chips,)), sem((chips,)), sem((chips,)),
             sem((chips,)), sem((chips,)),
-            sem((chips,)), sem((chips,)),
+            sem((chips - 1, group_axis)), sem((chips - 1, group_axis)),
             sem((group_axis,)), sem((group_axis,)),
             sem((lemma_axis,)), sem((lemma_axis,)),
             sem, sem,

time: 37.2 us -> 37.1 us (level)
  no operation moved by 1% of the time
where the time goes in v4:
time: 37.1 us; the launch traced here: 36.9 us
  Pallas kernels  36.2 us (98%)
  between operations  0.64 us (2%)
    pallas_call x1, Pallas kernels, fused_body(): pl.pallas_call(functools.partial(fused_kernel, lemma_axis, group_axis, le...  34.3 us
    pallas_call x1, Pallas kernels, fused_body(): pl.pallas_call(place_kernel, out_shape=(jax.ShapeDtypeStruct((states_dev,...  1.88 us

profile of v4, /device:TPU:0, one launch (start us, length us, event | category | flops | bytes accessed | tf_op | source)
XLA Modules:
  0.0 36.9 jit_solution(2738184685316999393)
XLA Ops:
  0.6 34.3 %shard_map.102 = (f32[1,128]{1,0:T(1,128)}, bf16[128,1536]{1,0:T(8,128)(2,1)}, f32[384,128]{1,0:T(8,128)}, f32[1,384]{1,0:T(1,128)}) custom-call(bf16[128,1536]{1,0:T(8,128)(2,1)} %bitcast.3, f32[1536]{0:T(1024)} %gain_ref.1, bf16[384,128]{1,0:T(8,128)(2,1)} %weight_ref.1, bf16[512,128]{1,0:T(8,128)(2,1)} %bitcast.5, s32[128]{0:T(128)} %len_ref.1, ...), custom_call_target="tpu_custom_call" | custom-call | flops 687865856 | bytes 1572864 | tf_op jit(solution)/shard_map/pallas_call | solution.py:526
  35.0 1.9 %shard_map.103 = (f32[2]{0:T(128)}, bf16[128,1536]{1,0:T(8,128)(2,1)}, f32[384,128]{1,0:T(8,128)}, f32[384]{0:T(512)}) custom-call(f32[1,128]{1,0:T(1,128)} %get-tuple-element.12.loss, bf16[128,1536]{1,0:T(8,128)(2,1)} %get-tuple-element.13.hgrad, f32[384,128]{1,0:T(8,128)} %get-tuple-element.14.wgrad, f32[1,384]{1,0:T(1,128)} %get-tuple-element.15.ggrad), custom_call_target="tpu_custom_call" | custom-call | tf_op jit(solution)/shard_map/pallas_call | solution.py:580

commit v5 on v4

--- a/solution.py
+++ b/solution.py
@@ -169,7 +169,6 @@
     chip, core = me // 2, lax.rem(me, 2)
     pair = chip * 2 + (1 - core)
     rows, width = hid.shape
-    gain_row = gain_ref[...].reshape(1, width)
     proj_width = weight_ref.shape[1]
     wrows = weight_ref.shape[0]
     hrows = wrows // 2
@@ -180,12 +179,17 @@
     along = chips // across
     chip_y, chip_x = chip // across, lax.rem(chip, across)
 
+    def split(step):
+        if isinstance(step, int):
+            return step // across, step % across
+        return lax.div(step, across), lax.rem(step, across)
+
     def chip_to(step):
-        step_y, step_x = step // across, step % across
+        step_y, step_x = split(step)
         return lax.rem(chip_y + step_y, along) * across + lax.rem(chip_x + step_x, across)
 
     def chip_source(step):
-        step_y, step_x = step // across, step % across
+        step_y, step_x = split(step)
         return lax.rem(chip_y + along - step_y, along) * across + lax.rem(
             chip_x + across - step_x, across
         )
@@ -265,7 +269,8 @@
     lengths_t = jnp.broadcast_to(
         lengths.astype(jnp.float32), (lemmas_all, lemmas_all)
     ).T[:, :1].astype(jnp.int32)
-    for block in range(chips):
+    @pl.loop(0, chips)
+    def _(block):
         first = -block * chip_tok
         member = (token_of >= first) & (token_of < lengths + first)
         live[block] = jnp.where(member, 1.0, 0.0).astype(jnp.bfloat16)
@@ -273,16 +278,29 @@
         live_t[block] = jnp.where(member, 1.0, 0.0).astype(jnp.bfloat16)
 
     hid_copy.wait()
-    in_float = hid[...].astype(jnp.float32)
-    inv_rms = lax.rsqrt(jnp.mean(in_float * in_float, axis=1, keepdims=True) + norm_eps)
-    scaled = (in_float * inv_rms * gain_row).astype(jnp.bfloat16)
-    scaled_b[...] = scaled
-    scaled_rows = scaled.T
     piece = wrows // lemma_axis
-    for group in range(group_axis):
+
+    def group_cols(group):
+        return pl.ds(pl.multiple_of(group * wrows, 128), wrows)
+
+    def add_squares(group, acc):
+        in_float = hid[:, group_cols(group)].astype(jnp.float32)
+        return acc + jnp.sum(in_float * in_float, axis=1, keepdims=True)
+
+    mean_sq = lax.fori_loop(0, group_axis, add_squares, jnp.zeros((rows, 1), jnp.float32)) / width
+    inv_rms = lax.rsqrt(mean_sq + norm_eps)
+
+    @pl.loop(0, group_axis)
+    def _(group):
+        cols = group_cols(group)
+        in_float = hid[:, cols].astype(jnp.float32)
+        scaled = (in_float * inv_rms * gain_ref[cols].reshape(1, wrows)).astype(jnp.bfloat16)
+        scaled_b[group] = scaled
+        scaled_rows = scaled.T
         for owner in range(lemma_axis):
-            start = group * wrows + owner * piece
-            scaled_t[owner // 2, owner % 2, group] = scaled_rows[start : start + piece]
+            scaled_t[owner // 2, owner % 2, group] = scaled_rows[
+                owner * piece : (owner + 1) * piece
+            ]
 
     own_gain = gain_ref[pl.ds(pl.multiple_of(grp * wrows, 128), wrows)].reshape(1, wrows)
     gain_col = jnp.broadcast_to(own_gain, (proj_width, wrows)).T
@@ -300,8 +318,12 @@
         dst = w_all.at[grp_from(step), other_half]
         remote(dst, dst, wf_send.at[step], wf_recv.at[step], pair, grp).wait_recv()
 
-    weight = w_all[...].reshape(width, proj_width)
-    projected = jnp.dot(scaled_b[...], weight, preferred_element_type=jnp.float32)
+    def project(group, acc):
+        return acc + jnp.dot(scaled_b[group], w_all[group], preferred_element_type=jnp.float32)
+
+    projected = lax.fori_loop(
+        0, group_axis, project, jnp.zeros((rows, proj_width), jnp.float32)
+    )
     proj_scale = lax.rsqrt(
         jnp.mean(projected * projected, axis=1, keepdims=True) + norm_eps
     ) / math.sqrt(proj_width)
@@ -318,22 +340,19 @@
     def forward(step):
         dst = keys.at[chip_source(step), core]
         remote(dst, dst, k_send.at[step], k_recv.at[step], chip_peer(step), grp).wait_recv()
-        copy = remote(dst, dst, kf_send.at[step], kf_recv.at[step], pair, grp)
-        copy.start()
-        kf_out.append(copy)
+        remote(dst, dst, kf_send.at[step], kf_recv.at[step], pair, grp).start()
 
     def chip_pass(step, total):
+        @pl.when(step + 1 < chips)
+        def _():
+            forward(step + 1)
+
         source = chip_source(step)
         dst = keys.at[source, 1 - core]
         remote(dst, dst, kf_send.at[step], kf_recv.at[step], pair, grp).wait_recv()
         return first_pass(source, total)
 
-    total = chip_pass(0, jnp.zeros((rows, lemmas_all), jnp.float32))
-    for step in range(1, chips):
-        forward(step)
-        if step > 1:
-            total = chip_pass(step - 1, total)
-    total = chip_pass(chips - 1, total)
+    total = lax.fori_loop(0, chips, chip_pass, jnp.zeros((rows, lemmas_all), jnp.float32))
 
     tok_lse = token_temp * jnp.log(total)
     first_state = (me * group_axis + grp) * states_dev
@@ -360,13 +379,14 @@
     loss_ref[...] = losses
     ratio = jnp.concatenate(ratios, axis=0).astype(jnp.bfloat16)
 
-    unit_grad = jnp.zeros((rows, proj_width), jnp.float32)
-    for block in range(chips):
+    def second_pass(block, acc):
         spread = jnp.dot(ratio, live_t[block], preferred_element_type=jnp.float32)
         coef = (powers_b[block].astype(jnp.float32) * spread).astype(jnp.bfloat16)
-        unit_grad += jnp.dot(
+        return acc + jnp.dot(
             coef, keys[block].reshape(chip_tok, proj_width), preferred_element_type=jnp.float32
         )
+
+    unit_grad = lax.fori_loop(0, chips, second_pass, jnp.zeros((rows, proj_width), jnp.float32))
     proj_grad = proj_scale * unit_grad - projected * (
         proj_scale * proj_scale * proj_scale
     ) * jnp.sum(projected * unit_grad, axis=1, keepdims=True)
@@ -378,53 +398,56 @@
             group_axis, piece, proj_width
         )
 
-    order = list(reversed(range(chips)))
-    p_out = []
-    for step in order:
+    def pair_copy(step):
+        return remote(
+            part.at[step], pair_in.at[step], p_send.at[step], p_recv.at[step], pair, grp
+        )
+
+    def chip_copy(step, grp_step):
+        return remote(
+            half.at[step, grp_peer(grp_step)], chip_in.at[step - 1, grp_step],
+            c_send.at[step - 1, grp_step], c_recv.at[step - 1, grp_step],
+            chip_peer(step), grp,
+        )
+
+    @pl.loop(0, chips)
+    def _(turn):
+        step = chips - 1 - turn
         part[step] = weight_part(chip_to(step), 1 - core).astype(jnp.bfloat16)
-        copy = remote(part.at[step], pair_in.at[step], p_send.at[step], p_recv.at[step], pair, grp)
-        copy.start()
-        p_out.append(copy)
-    grp_order = list(reversed(range(group_axis)))
-    c_out = {}
-    for step, pair_copy in zip(order, p_out):
+        pair_copy(step).start()
+
+    @pl.loop(0, chips)
+    def _(turn):
+        step = chips - 1 - turn
         mine = weight_part(chip_to(step), core)
-        pair_copy.wait_recv()
+        pair_copy(step).wait_recv()
         half[step] = (mine + pair_in[step].astype(jnp.float32)).astype(jnp.bfloat16)
-        if step:
-            for grp_step in grp_order:
-                copy = remote(
-                    half.at[step, grp_peer(grp_step)], chip_in.at[step - 1, grp_step],
-                    c_send.at[step - 1, grp_step], c_recv.at[step - 1, grp_step],
-                    chip_peer(step), grp,
-                )
-                copy.start()
-                c_out[step, grp_step] = copy
+
+        @pl.when(step > 0)
+        def _():
+            for grp_step in reversed(range(group_axis)):
+                chip_copy(step, grp_step).start()
 
     row_dot = jnp.sum(projected * proj_grad_b.astype(jnp.float32), axis=1, keepdims=True)
     row_scale = inv_rms * inv_rms * row_dot / width
 
-    def hidden_part(state):
-        span = slice(state * query_tok, (state + 1) * query_tok)
+    def hidden_part(group):
+        cols = group_cols(group)
         scaled_grad = lax.dot_general(
-            proj_grad_b[span], w_all[...].reshape(width, proj_width), NT,
-            preferred_element_type=jnp.float32,
-        )
-        hout[span] = (
-            inv_rms[span] * (scaled_grad * gain_row)
-            - hid[span].astype(jnp.float32) * row_scale[span]
+            proj_grad_b, w_all[group], NT, preferred_element_type=jnp.float32
+        )
+        hout[:, cols] = (
+            inv_rms * (scaled_grad * gain_ref[cols].reshape(1, wrows))
+            - hid[:, cols].astype(jnp.float32) * row_scale
         ).astype(jnp.bfloat16)
-        copy = pltpu.make_async_copy(hout.at[span], hgrad_ref.at[span], local_sem.at[3 + state])
-        copy.start()
-        return copy
-
-    hout_copies = [hidden_part(0)]
+
+    pl.loop(0, group_axis // 2)(hidden_part)
 
     g_out = []
-    for grp_step in grp_order:
+    for grp_step in reversed(range(group_axis)):
         chip_sum = half[0, grp_peer(grp_step)].astype(jnp.float32)
         for step in range(1, chips):
-            c_out[step, grp_step].wait_recv()
+            chip_copy(step, grp_step).wait_recv()
             chip_sum += chip_in[step - 1, grp_step].astype(jnp.float32)
         if grp_step:
             quarter[grp_step] = chip_sum.astype(jnp.bfloat16)
@@ -436,7 +459,9 @@
             g_out.append(copy)
         else:
             grp_sum = chip_sum
-    hout_copies += [hidden_part(state) for state in range(1, states_dev)]
+    pl.loop(group_axis // 2, group_axis)(hidden_part)
+    hout_copy = pltpu.make_async_copy(hout, hgrad_ref, local_sem.at[3])
+    hout_copy.start()
     for copy in g_out:
         copy.wait_recv()
     for step in range(1, group_axis):
@@ -479,10 +504,16 @@
     wgrad_ref[...] = weight_raw * factor
     ggrad_ref[...] = gain_raw * factor[:, :1]
 
-    for copy in w_out + k_out + wf_out + kf_out + p_out + list(c_out.values()) + g_out + a_out:
+    for copy in w_out + k_out + wf_out + kf_out + g_out + a_out:
         copy.wait_send()
-    for copy in hout_copies:
-        copy.wait()
+    for step in range(chips):
+        pair_copy(step).wait_send()
+        if step:
+            dst = keys.at[chip_source(step), core]
+            remote(dst, dst, kf_send.at[step], kf_recv.at[step], pair, grp).wait_send()
+            for grp_step in range(group_axis):
+                chip_copy(step, grp_step).wait_send()
+    hout_copy.wait()
 
 
 def place_kernel(
@@ -544,7 +575,7 @@
             pltpu.VMEM((chips, 2 * block_tok, lemmas_all), bf16),
             pltpu.VMEM((chips, lemmas_all, 2 * block_tok), bf16),
             pltpu.VMEM((chips, rows, 2 * block_tok), bf16),
-            pltpu.VMEM((rows, width), bf16),
+            pltpu.VMEM((group_axis, rows, wrows), bf16),
             pltpu.VMEM((chips, 2, group_axis, piece, rows), bf16),
             pltpu.VMEM((chips, group_axis, piece, proj_width), bf16),
             pltpu.VMEM((chips, group_axis, piece, proj_width), bf16),
@@ -555,7 +586,7 @@
             pltpu.VMEM((lemma_axis, piece, proj_width), bf16),
             pltpu.VMEM((group_axis * lemma_axis, 1, 128), f32),
             pltpu.VMEM((lemma_axis, piece, proj_width), f32),
-            sem((3 + states_dev,)),
+            sem((4,)),
             sem((group_axis,)), sem((group_axis,)), sem((group_axis,)), sem((group_axis,)),
             sem((chips,)), sem((chips,)), sem((chips,)), sem((chips,)),
             sem((chips,)), sem((chips,)),

time: 37.1 us -> 37.6 us (1.013)
  Pallas kernels: 36.2 us -> 36.7 us
    pallas_call x1, Pallas kernels: 34.3 us -> 34.8 us  [fused_body(): pl.pallas_call(functools.partial(fused_kernel, lemma_axis, group_axis, le...]
where the time goes in v5:
time: 37.6 us; the launch traced here: 37.4 us
  Pallas kernels  36.7 us (98%)
  between operations  0.64 us (2%)
    pallas_call x1, Pallas kernels, fused_body(): pl.pallas_call(functools.partial(fused_kernel, lemma_axis, group_axis, le...  34.8 us
    pallas_call x1, Pallas kernels, fused_body(): pl.pallas_call(place_kernel, out_shape=(jax.ShapeDtypeStruct((states_dev,...  1.88 us

profile of v5, /device:TPU:0, one launch (start us, length us, event | category | flops | bytes accessed | tf_op | source)
XLA Modules:
  0.0 37.4 jit_solution(13634730512806167348)
XLA Ops:
  0.6 34.8 %shard_map.102 = (f32[1,128]{1,0:T(1,128)}, bf16[128,1536]{1,0:T(8,128)(2,1)}, f32[384,128]{1,0:T(8,128)}, f32[1,384]{1,0:T(1,128)}) custom-call(bf16[128,1536]{1,0:T(8,128)(2,1)} %bitcast.3, f32[1536]{0:T(1024)} %gain_ref.1, bf16[384,128]{1,0:T(8,128)(2,1)} %weight_ref.1, bf16[512,128]{1,0:T(8,128)(2,1)} %bitcast.5, s32[128]{0:T(128)} %len_ref.1, ...), custom_call_target="tpu_custom_call" | custom-call | flops 687865856 | bytes 1572864 | tf_op jit(solution)/shard_map/pallas_call | solution.py:557
  35.5 1.9 %shard_map.103 = (f32[2]{0:T(128)}, bf16[128,1536]{1,0:T(8,128)(2,1)}, f32[384,128]{1,0:T(8,128)}, f32[384]{0:T(512)}) custom-call(f32[1,128]{1,0:T(1,128)} %get-tuple-element.12.loss, bf16[128,1536]{1,0:T(8,128)(2,1)} %get-tuple-element.13.hgrad, f32[384,128]{1,0:T(8,128)} %get-tuple-element.14.wgrad, f32[1,384]{1,0:T(1,128)} %get-tuple-element.15.ggrad), custom_call_target="tpu_custom_call" | custom-call | tf_op jit(solution)/shard_map/pallas_call | solution.py:611

commit v6 on v5

--- a/solution.py
+++ b/solution.py
@@ -224,7 +224,7 @@
         (lemma_step, grp_step)
         for lemma_step in range(lemma_axis)
         for grp_step in range(group_axis)
-        if lemma_step or grp_step
+        if (lemma_step == 0) != (grp_step == 0)
     ]
     for lemma_step, grp_step in others:
         pl.semaphore_signal(
@@ -466,8 +466,7 @@
         copy.wait_recv()
     for step in range(1, group_axis):
         grp_sum += grp_in[step - 1].astype(jnp.float32)
-    own_raw = grp_sum.astype(jnp.bfloat16)
-    raw[me] = own_raw
+    raw[me] = grp_sum.astype(jnp.bfloat16)
     a_out = []
     for step in range(1, lemma_axis):
         copy = remote(
@@ -476,17 +475,6 @@
         )
         copy.start()
         a_out.append(copy)
-    own_raw = own_raw.astype(jnp.float32)
-    own_gain_raw = jnp.sum(own_raw * over_gain[me], axis=1, keepdims=True)
-    squares = jnp.sum(own_raw * own_raw) + jnp.sum(own_gain_raw * own_gain_raw)
-    my_sq = sq.at[grp * lemma_axis + me]
-    my_sq[...] = jnp.full((1, 128), squares, jnp.float32)
-    for lemma_step, grp_step in others:
-        copy = remote(
-            my_sq, my_sq, s_send, s_recv,
-            lax.rem(me + lemma_step, lemma_axis), grp_peer(grp_step),
-        )
-        copy.start()
     for step in range(1, lemma_axis):
         dst = raw.at[lax.rem(me + lemma_axis - step, lemma_axis)]
         remote(dst, dst, a_send.at[step], a_recv.at[step], pair, grp).wait_recv()
@@ -497,14 +485,25 @@
         ones, over_gain[...].reshape(wrows, proj_width) * weight_raw, NT,
         preferred_element_type=jnp.float32, precision=lax.Precision.HIGHEST,
     )[:1]
-    all_but_one = sq.at[pl.ds(0, len(others))]
-    remote(all_but_one, all_but_one, s_send, s_recv, pair, grp).wait()
+    squares = jnp.sum(
+        jnp.sum(weight_raw * weight_raw, axis=0, keepdims=True), axis=1, keepdims=True
+    ) + jnp.sum(gain_raw * gain_raw, axis=1, keepdims=True)
+    my_sq = sq.at[grp]
+    my_sq[...] = jnp.broadcast_to(squares, (1, 128))
+    s_out = []
+    for step in range(1, group_axis):
+        copy = remote(my_sq, my_sq, s_send.at[step], s_recv.at[step], me, grp_peer(step))
+        copy.start()
+        s_out.append(copy)
+    for step in range(1, group_axis):
+        dst = sq.at[grp_from(step)]
+        remote(dst, dst, s_send.at[step], s_recv.at[step], me, grp_peer(step)).wait_recv()
     squares_all = jnp.sum(sq[...], axis=0)
     factor = jnp.minimum(1.0, grad_limit / jnp.sqrt(squares_all + norm_eps))
     wgrad_ref[...] = weight_raw * factor
     ggrad_ref[...] = gain_raw * factor[:, :1]
 
-    for copy in w_out + k_out + wf_out + kf_out + g_out + a_out:
+    for copy in w_out + k_out + wf_out + kf_out + g_out + a_out + s_out:
         copy.wait_send()
     for step in range(chips):
         pair_copy(step).wait_send()
@@ -584,7 +583,7 @@
             pltpu.VMEM((group_axis, piece, proj_width), bf16),
             pltpu.VMEM((group_axis - 1, piece, proj_width), bf16),
             pltpu.VMEM((lemma_axis, piece, proj_width), bf16),
-            pltpu.VMEM((group_axis * lemma_axis, 1, 128), f32),
+            pltpu.VMEM((group_axis, 1, 128), f32),
             pltpu.VMEM((lemma_axis, piece, proj_width), f32),
             sem((4,)),
             sem((group_axis,)), sem((group_axis,)), sem((group_axis,)), sem((group_axis,)),
@@ -593,7 +592,7 @@
             sem((chips - 1, group_axis)), sem((chips - 1, group_axis)),
             sem((group_axis,)), sem((group_axis,)),
             sem((lemma_axis,)), sem((lemma_axis,)),
-            sem, sem,
+            sem((group_axis,)), sem((group_axis,)),
         ],
         compiler_params=pltpu.CompilerParams(
             collective_id=0, has_side_effects=True, vmem_limit_bytes=62 * 1024 * 1024

time: 37.6 us -> 38.3 us (1.019)
  Pallas kernels: 36.7 us -> 37.4 us
    pallas_call x1, Pallas kernels: 34.8 us -> 35.6 us  [fused_body(): pl.pallas_call(functools.partial(fused_kernel, lemma_axis, group_axis, le...]
where the time goes in v6:
time: 38.3 us; the launch traced here: 38.1 us
  Pallas kernels  37.4 us (98%)
  between operations  0.64 us (2%)
    pallas_call x1, Pallas kernels, fused_body(): pl.pallas_call(functools.partial(fused_kernel, lemma_axis, group_axis, le...  35.6 us
    pallas_call x1, Pallas kernels, fused_body(): pl.pallas_call(place_kernel, out_shape=(jax.ShapeDtypeStruct((states_dev,...  1.88 us

profile of v6, /device:TPU:0, one launch (start us, length us, event | category | flops | bytes accessed | tf_op | source)
XLA Modules:
  0.0 38.1 jit_solution(12359942224791607725)
XLA Ops:
  0.6 35.6 %shard_map.102 = (f32[1,128]{1,0:T(1,128)}, bf16[128,1536]{1,0:T(8,128)(2,1)}, f32[384,128]{1,0:T(8,128)}, f32[1,384]{1,0:T(1,128)}) custom-call(bf16[128,1536]{1,0:T(8,128)(2,1)} %bitcast.3, f32[1536]{0:T(1024)} %gain_ref.1, bf16[384,128]{1,0:T(8,128)(2,1)} %weight_ref.1, bf16[512,128]{1,0:T(8,128)(2,1)} %bitcast.5, s32[128]{0:T(128)} %len_ref.1, ...), custom_call_target="tpu_custom_call" | custom-call | flops 687865856 | bytes 1572864 | tf_op jit(solution)/shard_map/pallas_call | solution.py:556
  36.2 1.9 %shard_map.103 = (f32[2]{0:T(128)}, bf16[128,1536]{1,0:T(8,128)(2,1)}, f32[384,128]{1,0:T(8,128)}, f32[384]{0:T(512)}) custom-call(f32[1,128]{1,0:T(1,128)} %get-tuple-element.12.loss, bf16[128,1536]{1,0:T(8,128)(2,1)} %get-tuple-element.13.hgrad, f32[384,128]{1,0:T(8,128)} %get-tuple-element.14.wgrad, f32[1,384]{1,0:T(1,128)} %get-tuple-element.15.ggrad), custom_call_target="tpu_custom_call" | custom-call | tf_op jit(solution)/shard_map/pallas_call | solution.py:610

commit v7 on v4

--- a/solution.py
+++ b/solution.py
@@ -157,11 +157,12 @@
 
 def fused_kernel(
     lemma_axis, group_axis, lemma_dev, lemma_tok, states_dev, query_tok,
-    hidden_ref, gain_ref, weight_ref, emb_ref, len_ref, qlen_ref, pos_ref,
-    loss_ref, hgrad_ref, wgrad_ref, ggrad_ref,
+    hidden_ref, gain_hbm, weight_ref, emb_ref, len_hbm, qlen_hbm, pos_hbm,
+    loss_ref, hgrad_ref, raw_ref, ggrad_ref, factor_ref,
+    gain_ref, len_ref, qlen_ref, pos_ref, loss_row, gain_out, factor_row,
     hid, emb, hout, w_all, keys, live, live_t, powers_b, scaled_b, scaled_t,
     part, pair_in, half, chip_in, quarter, grp_in, raw, sq, over_gain,
-    local_sem, w_send, w_recv, wf_send, wf_recv, k_send, k_recv, kf_send, kf_recv,
+    local_sem, table_sem, w_send, w_recv, wf_send, wf_recv, k_send, k_recv, kf_send, kf_recv,
     p_send, p_recv, c_send, c_recv, g_send, g_recv, a_send, a_recv, s_send, s_recv,
 ):
     chips = lemma_axis // 2
@@ -169,7 +170,6 @@
     chip, core = me // 2, lax.rem(me, 2)
     pair = chip * 2 + (1 - core)
     rows, width = hid.shape
-    gain_row = gain_ref[...].reshape(1, width)
     proj_width = weight_ref.shape[1]
     wrows = weight_ref.shape[0]
     hrows = wrows // 2
@@ -213,7 +213,6 @@
     w_copy = pltpu.make_async_copy(weight_ref, w_all.at[grp], local_sem.at[2])
     emb_copy.start()
     w_copy.start()
-    hid_copy.start()
 
     barrier = pltpu.get_barrier_semaphore()
     others = [
@@ -228,6 +227,16 @@
             device_id=(lax.rem(me + lemma_step, lemma_axis), grp_peer(grp_step)),
         )
 
+    tables = [
+        pltpu.make_async_copy(src, dst, table_sem.at[index])
+        for index, (src, dst) in enumerate(
+            [(len_hbm, len_ref), (gain_hbm, gain_ref), (qlen_hbm, qlen_ref), (pos_hbm, pos_ref)]
+        )
+    ]
+    hid_copy.start()
+    for copy in tables:
+        copy.start()
+
     emb_copy.wait()
     tokens = emb[...].astype(jnp.float32)
     token_scale = lax.rsqrt(
@@ -254,6 +263,9 @@
     kf_out = [remote(keys.at[chip, core], keys.at[chip, core], kf_send.at[0], kf_recv.at[0], pair, grp)]
     kf_out[0].start()
 
+    for copy in tables:
+        copy.wait()
+    gain_row = gain_ref[...].reshape(1, width)
     chip_tok = 2 * block_tok
     token_of = lax.broadcasted_iota(
         jnp.int32, (chip_tok, lemmas_all), 0
@@ -357,7 +369,9 @@
         losses = jnp.where(lane == state, loss, losses)
         grad_sim = loss_scale * (powers / partition - is_positive) / state_temp
         ratios.append(live_rows * (grad_sim / length_f) / total[span])
-    loss_ref[...] = losses
+    loss_row[...] = losses
+    loss_copy = pltpu.make_async_copy(loss_row, loss_ref, table_sem.at[4])
+    loss_copy.start()
     ratio = jnp.concatenate(ratios, axis=0).astype(jnp.bfloat16)
 
     unit_grad = jnp.zeros((rows, proj_width), jnp.float32)
@@ -443,6 +457,17 @@
         grp_sum += grp_in[step - 1].astype(jnp.float32)
     own_raw = grp_sum.astype(jnp.bfloat16)
     raw[me] = own_raw
+    own_raw = own_raw.astype(jnp.float32)
+    own_gain_raw = jnp.sum(own_raw * over_gain[me], axis=1, keepdims=True)
+    squares = jnp.sum(own_raw * own_raw) + jnp.sum(own_gain_raw * own_gain_raw)
+    my_sq = sq.at[grp * lemma_axis + me]
+    my_sq[...] = jnp.full((1, 128), squares, jnp.float32)
+    for lemma_step, grp_step in reversed(others):
+        copy = remote(
+            my_sq, my_sq, s_send, s_recv,
+            lax.rem(me + lemma_step, lemma_axis), grp_peer(grp_step),
+        )
+        copy.start()
     a_out = []
     for step in range(1, lemma_axis):
         copy = remote(
@@ -451,60 +476,57 @@
         )
         copy.start()
         a_out.append(copy)
-    own_raw = own_raw.astype(jnp.float32)
-    own_gain_raw = jnp.sum(own_raw * over_gain[me], axis=1, keepdims=True)
-    squares = jnp.sum(own_raw * own_raw) + jnp.sum(own_gain_raw * own_gain_raw)
-    my_sq = sq.at[grp * lemma_axis + me]
-    my_sq[...] = jnp.full((1, 128), squares, jnp.float32)
-    for lemma_step, grp_step in others:
-        copy = remote(
-            my_sq, my_sq, s_send, s_recv,
-            lax.rem(me + lemma_step, lemma_axis), grp_peer(grp_step),
-        )
-        copy.start()
     for step in range(1, lemma_axis):
         dst = raw.at[lax.rem(me + lemma_axis - step, lemma_axis)]
         remote(dst, dst, a_send.at[step], a_recv.at[step], pair, grp).wait_recv()
 
+    raw_copy = pltpu.make_async_copy(raw, raw_ref, table_sem.at[5])
+    raw_copy.start()
     weight_raw = raw[...].reshape(wrows, proj_width).astype(jnp.float32)
     ones = jnp.ones((8, proj_width), jnp.float32)
     gain_raw = lax.dot_general(
         ones, over_gain[...].reshape(wrows, proj_width) * weight_raw, NT,
         preferred_element_type=jnp.float32, precision=lax.Precision.HIGHEST,
     )[:1]
+    gain_out[...] = gain_raw
+    gain_copy = pltpu.make_async_copy(gain_out, ggrad_ref, table_sem.at[6])
+    gain_copy.start()
     all_but_one = sq.at[pl.ds(0, len(others))]
     remote(all_but_one, all_but_one, s_send, s_recv, pair, grp).wait()
     squares_all = jnp.sum(sq[...], axis=0)
     factor = jnp.minimum(1.0, grad_limit / jnp.sqrt(squares_all + norm_eps))
-    wgrad_ref[...] = weight_raw * factor
-    ggrad_ref[...] = gain_raw * factor[:, :1]
+    factor_row[...] = factor
+    factor_copy = pltpu.make_async_copy(factor_row, factor_ref, table_sem.at[7])
+    factor_copy.start()
 
     for copy in w_out + k_out + wf_out + kf_out + p_out + list(c_out.values()) + g_out + a_out:
         copy.wait_send()
-    for copy in hout_copies:
+    for copy in hout_copies + [loss_copy, raw_copy, gain_copy, factor_copy]:
         copy.wait()
 
 
 def place_kernel(
-    loss, hgrad, wgrad, ggrad, loss_out, hgrad_out, wgrad_out, ggrad_out,
-    loss_in, hbuf, wbuf, ggrad_in, loss_row, ggrad_row, sems,
+    loss, hgrad, raw, gain_raw, factor, loss_out, hgrad_out, wgrad_out, ggrad_out,
+    loss_in, hbuf, raw_in, gain_in, factor_in, loss_row, wbuf, ggrad_row, sems,
 ):
-    pairs = [(hgrad, hbuf), (wgrad, wbuf), (loss, loss_in), (ggrad, ggrad_in)]
+    pairs = [(factor, factor_in), (raw, raw_in), (gain_raw, gain_in), (loss, loss_in), (hgrad, hbuf)]
     copies = [pltpu.make_async_copy(a, b, sems.at[i]) for i, (a, b) in enumerate(pairs)]
     for copy in copies:
         copy.start()
-    pairs = [(hbuf, hgrad_out), (wbuf, wgrad_out), (loss_row, loss_out), (ggrad_row, ggrad_out)]
-    backs = [pltpu.make_async_copy(a, b, sems.at[4 + i]) for i, (a, b) in enumerate(pairs)]
+    pairs = [(wbuf, wgrad_out), (ggrad_row, ggrad_out), (loss_row, loss_out), (hbuf, hgrad_out)]
+    backs = [pltpu.make_async_copy(a, b, sems.at[5 + i]) for i, (a, b) in enumerate(pairs)]
+    copies[4].wait()
+    backs[3].start()
     copies[0].wait()
+    copies[1].wait()
+    wbuf[...] = raw_in[...].reshape(wbuf.shape).astype(jnp.float32) * factor_in[...]
     backs[0].start()
-    copies[1].wait()
+    copies[2].wait()
+    ggrad_row[...] = (gain_in[...] * factor_in[:, :1]).reshape(ggrad_row.shape)
     backs[1].start()
-    copies[2].wait()
+    copies[3].wait()
     loss_row[...] = loss_in[0, : loss_row.shape[0]]
     backs[2].start()
-    copies[3].wait()
-    ggrad_row[...] = ggrad_in[...].reshape(ggrad_row.shape)
-    backs[3].start()
     for copy in backs:
         copy.wait()
 
@@ -518,8 +540,6 @@
     rows, block_tok = states_dev * query_tok, lemma_dev * lemma_tok
     piece = wrows // lemma_axis
     lemmas_all = lemma_dev * lemma_axis
-    vmem = pl.BlockSpec(memory_space=pltpu.VMEM)
-    smem = pl.BlockSpec(memory_space=pltpu.SMEM)
     hbm = pl.BlockSpec(memory_space=pltpu.HBM)
     sem = pltpu.SemaphoreType.DMA
     bf16, f32 = jnp.bfloat16, jnp.float32
@@ -530,12 +550,20 @@
         out_shape=(
             jax.ShapeDtypeStruct((1, 128), f32),
             jax.ShapeDtypeStruct((rows, width), bf16),
-            jax.ShapeDtypeStruct((wrows, proj_width), f32),
+            jax.ShapeDtypeStruct((lemma_axis, piece, proj_width), bf16),
             jax.ShapeDtypeStruct((1, wrows), f32),
+            jax.ShapeDtypeStruct((1, 128), f32),
         ),
-        in_specs=[hbm, vmem, hbm, hbm, vmem, smem, smem],
-        out_specs=(vmem, hbm, vmem, vmem),
+        in_specs=[hbm] * 7,
+        out_specs=(hbm,) * 5,
         scratch_shapes=[
+            pltpu.VMEM((width,), f32),
+            pltpu.VMEM((lemmas_all,), jnp.int32),
+            pltpu.SMEM(query_len.shape, jnp.int32),
+            pltpu.SMEM(positive.shape, jnp.int32),
+            pltpu.VMEM((1, 128), f32),
+            pltpu.VMEM((1, wrows), f32),
+            pltpu.VMEM((1, 128), f32),
             pltpu.VMEM((rows, width), bf16),
             pltpu.VMEM((block_tok, proj_width), bf16),
             pltpu.VMEM((rows, width), bf16),
@@ -555,7 +583,7 @@
             pltpu.VMEM((lemma_axis, piece, proj_width), bf16),
             pltpu.VMEM((group_axis * lemma_axis, 1, 128), f32),
             pltpu.VMEM((lemma_axis, piece, proj_width), f32),
-            sem((3 + states_dev,)),
+            sem((3 + states_dev,)), sem((8,)),
             sem((group_axis,)), sem((group_axis,)), sem((group_axis,)), sem((group_axis,)),
             sem((chips,)), sem((chips,)), sem((chips,)), sem((chips,)),
             sem((chips,)), sem((chips,)),
@@ -585,16 +613,18 @@
             jax.ShapeDtypeStruct((wrows, proj_width), f32),
             jax.ShapeDtypeStruct((wrows,), f32),
         ),
-        in_specs=[hbm] * 4,
+        in_specs=[hbm] * 5,
         out_specs=(hbm,) * 4,
         scratch_shapes=[
             pltpu.VMEM((1, 128), f32),
             pltpu.VMEM((rows, width), bf16),
+            pltpu.VMEM((lemma_axis, piece, proj_width), bf16),
+            pltpu.VMEM((1, wrows), f32),
+            pltpu.VMEM((1, 128), f32),
+            pltpu.VMEM((states_dev,), f32),
             pltpu.VMEM((wrows, proj_width), f32),
-            pltpu.VMEM((1, wrows), f32),
-            pltpu.VMEM((states_dev,), f32),
             pltpu.VMEM((wrows,), f32),
-            sem((8,)),
+            sem((9,)),
         ],
         compiler_params=pltpu.CompilerParams(vmem_limit_bytes=62 * 1024 * 1024),
     )(*outs)

time: 37.1 us -> 36.2 us (0.976)
  Pallas kernels: 36.2 us -> 35.4 us
    pallas_call x1, Pallas kernels: 34.3 us -> 33.4 us  [fused_body(): pl.pallas_call(functools.partial(fused_kernel, lemma_axis, group_axis, le...]
where the time goes in v7:
time: 36.2 us; the launch traced here: 36 us
  Pallas kernels  35.4 us (98%)
  between operations  0.64 us (2%)
    pallas_call x1, Pallas kernels, fused_body(): pl.pallas_call(functools.partial(fused_kernel, lemma_axis, group_axis, le...  33.4 us
    pallas_call x1, Pallas kernels, fused_body(): pl.pallas_call(place_kernel, out_shape=(jax.ShapeDtypeStruct((states_dev,...  1.95 us

profile of v7, /device:TPU:0, one launch (start us, length us, event | category | flops | bytes accessed | tf_op | source)
XLA Modules:
  0.0 36.0 jit_solution(12202170182227728549)
XLA Ops:
  0.6 33.4 %shard_map.102 = (f32[1,128]{1,0:T(1,128)}, bf16[128,1536]{1,0:T(8,128)(2,1)}, bf16[8,48,128]{2,1,0:T(8,128)(2,1)}, f32[1,384]{1,0:T(1,128)}, f32[1,128]{1,0:T(1,128)}) custom-call(bf16[128,1536]{1,0:T(8,128)(2,1)} %bitcast.3, f32[1536]{0:T(1024)} %gain_hbm.1, bf16[384,128]{1,0:T(8,128)(2,1)} %weight_ref.1, bf16[512,128]{1,0:T(8,128)(2,1)} %bitcast.5, ...), custom_call_target="tpu_custom_call" | custom-call | flops 687865856 | bytes 1572864 | tf_op jit(solution)/shard_map/pallas_call | solution.py:546
  34.1 2.0 %shard_map.103 = (f32[2]{0:T(128)}, bf16[128,1536]{1,0:T(8,128)(2,1)}, f32[384,128]{1,0:T(8,128)}, f32[384]{0:T(512)}) custom-call(f32[1,128]{1,0:T(1,128)} %get-tuple-element.13.loss, bf16[128,1536]{1,0:T(8,128)(2,1)} %get-tuple-element.14.hgrad, bf16[8,48,128]{2,1,0:T(8,128)(2,1)} %get-tuple-element.15.raw, f32[1,384]{1,0:T(1,128)} %get-tuple-element.16.gain_raw, ...), custom_call_target="tpu_custom_call" | custom-call | tf_op jit(solution)/shard_map/pallas_call | solution.py:608

commit v8 on v7

--- a/solution.py
+++ b/solution.py
@@ -307,6 +307,15 @@
         copy = remote(dst, dst, wf_send.at[step], wf_recv.at[step], pair, grp)
         copy.start()
         wf_out.append(copy)
+    def forward(step):
+        dst = keys.at[chip_source(step), core]
+        remote(dst, dst, k_send.at[step], k_recv.at[step], chip_peer(step), grp).wait_recv()
+        copy = remote(dst, dst, kf_send.at[step], kf_recv.at[step], pair, grp)
+        copy.start()
+        kf_out.append(copy)
+
+    for step in range(1, chips - 1):
+        forward(step)
     other_half = pl.ds(pl.multiple_of((1 - core) * hrows, hrows), hrows)
     for step in range(1, group_axis):
         dst = w_all.at[grp_from(step), other_half]
@@ -327,25 +336,16 @@
         powers_b[block] = exp_terms
         return total + jnp.dot(exp_terms, live[block], preferred_element_type=jnp.float32)
 
-    def forward(step):
-        dst = keys.at[chip_source(step), core]
-        remote(dst, dst, k_send.at[step], k_recv.at[step], chip_peer(step), grp).wait_recv()
-        copy = remote(dst, dst, kf_send.at[step], kf_recv.at[step], pair, grp)
-        copy.start()
-        kf_out.append(copy)
-
     def chip_pass(step, total):
         source = chip_source(step)
         dst = keys.at[source, 1 - core]
         remote(dst, dst, kf_send.at[step], kf_recv.at[step], pair, grp).wait_recv()
         return first_pass(source, total)
 
-    total = chip_pass(0, jnp.zeros((rows, lemmas_all), jnp.float32))
-    for step in range(1, chips):
-        forward(step)
-        if step > 1:
-            total = chip_pass(step - 1, total)
-    total = chip_pass(chips - 1, total)
+    forward(chips - 1)
+    total = jnp.zeros((rows, lemmas_all), jnp.float32)
+    for step in range(chips):
+        total = chip_pass(step, total)
 
     tok_lse = token_temp * jnp.log(total)
     first_state = (me * group_axis + grp) * states_dev

time: 36.2 us -> 35.3 us (0.975)
  Pallas kernels: 35.4 us -> 34.5 us
    pallas_call x1, Pallas kernels: 33.4 us -> 32.6 us  [fused_body(): pl.pallas_call(functools.partial(fused_kernel, lemma_axis, group_axis, le...]
where the time goes in v8:
time: 35.3 us; the launch traced here: 35.2 us
  Pallas kernels  34.5 us (98%)
  between operations  0.64 us (2%)
    pallas_call x1, Pallas kernels, fused_body(): pl.pallas_call(functools.partial(fused_kernel, lemma_axis, group_axis, le...  32.6 us
    pallas_call x1, Pallas kernels, fused_body(): pl.pallas_call(place_kernel, out_shape=(jax.ShapeDtypeStruct((states_dev,...  1.95 us

profile of v8, /device:TPU:0, one launch (start us, length us, event | category | flops | bytes accessed | tf_op | source)
XLA Modules:
  0.0 35.2 jit_solution(6035525456386507014)
XLA Ops:
  0.6 32.6 %shard_map.102 = (f32[1,128]{1,0:T(1,128)}, bf16[128,1536]{1,0:T(8,128)(2,1)}, bf16[8,48,128]{2,1,0:T(8,128)(2,1)}, f32[1,384]{1,0:T(1,128)}, f32[1,128]{1,0:T(1,128)}) custom-call(bf16[128,1536]{1,0:T(8,128)(2,1)} %bitcast.3, f32[1536]{0:T(1024)} %gain_hbm.1, bf16[384,128]{1,0:T(8,128)(2,1)} %weight_ref.1, bf16[512,128]{1,0:T(8,128)(2,1)} %bitcast.5, ...), custom_call_target="tpu_custom_call" | custom-call | flops 687865856 | bytes 1572864 | tf_op jit(solution)/shard_map/pallas_call | solution.py:546
  33.2 2.0 %shard_map.103 = (f32[2]{0:T(128)}, bf16[128,1536]{1,0:T(8,128)(2,1)}, f32[384,128]{1,0:T(8,128)}, f32[384]{0:T(512)}) custom-call(f32[1,128]{1,0:T(1,128)} %get-tuple-element.13.loss, bf16[128,1536]{1,0:T(8,128)(2,1)} %get-tuple-element.14.hgrad, bf16[8,48,128]{2,1,0:T(8,128)(2,1)} %get-tuple-element.15.raw, f32[1,384]{1,0:T(1,128)} %get-tuple-element.16.gain_raw, ...), custom_call_target="tpu_custom_call" | custom-call | tf_op jit(solution)/shard_map/pallas_call | solution.py:608

commit v9 on v8

--- a/solution.py
+++ b/solution.py
@@ -314,7 +314,7 @@
         copy.start()
         kf_out.append(copy)
 
-    for step in range(1, chips - 1):
+    for step in range(1, chips):
         forward(step)
     other_half = pl.ds(pl.multiple_of((1 - core) * hrows, hrows), hrows)
     for step in range(1, group_axis):
@@ -342,7 +342,6 @@
         remote(dst, dst, kf_send.at[step], kf_recv.at[step], pair, grp).wait_recv()
         return first_pass(source, total)
 
-    forward(chips - 1)
     total = jnp.zeros((rows, lemmas_all), jnp.float32)
     for step in range(chips):
         total = chip_pass(step, total)

time: 35.3 us -> 35.3 us (level)
  no operation moved by 1% of the time
where the time goes in v9:
time: 35.3 us; the launch traced here: 35.2 us
  Pallas kernels  34.5 us (98%)
  between operations  0.64 us (2%)
    pallas_call x1, Pallas kernels, fused_body(): pl.pallas_call(functools.partial(fused_kernel, lemma_axis, group_axis, le...  32.6 us
    pallas_call x1, Pallas kernels, fused_body(): pl.pallas_call(place_kernel, out_shape=(jax.ShapeDtypeStruct((states_dev,...  1.95 us

profile of v9, /device:TPU:0, one launch (start us, length us, event | category | flops | bytes accessed | tf_op | source)
XLA Modules:
  0.0 35.2 jit_solution(11757038930077611607)
XLA Ops:
  0.6 32.6 %shard_map.102 = (f32[1,128]{1,0:T(1,128)}, bf16[128,1536]{1,0:T(8,128)(2,1)}, bf16[8,48,128]{2,1,0:T(8,128)(2,1)}, f32[1,384]{1,0:T(1,128)}, f32[1,128]{1,0:T(1,128)}) custom-call(bf16[128,1536]{1,0:T(8,128)(2,1)} %bitcast.3, f32[1536]{0:T(1024)} %gain_hbm.1, bf16[384,128]{1,0:T(8,128)(2,1)} %weight_ref.1, bf16[512,128]{1,0:T(8,128)(2,1)} %bitcast.5, ...), custom_call_target="tpu_custom_call" | custom-call | flops 687865856 | bytes 1572864 | tf_op jit(solution)/shard_map/pallas_call | solution.py:545
  33.2 2.0 %shard_map.103 = (f32[2]{0:T(128)}, bf16[128,1536]{1,0:T(8,128)(2,1)}, f32[384,128]{1,0:T(8,128)}, f32[384]{0:T(512)}) custom-call(f32[1,128]{1,0:T(1,128)} %get-tuple-element.13.loss, bf16[128,1536]{1,0:T(8,128)(2,1)} %get-tuple-element.14.hgrad, bf16[8,48,128]{2,1,0:T(8,128)(2,1)} %get-tuple-element.15.raw, f32[1,384]{1,0:T(1,128)} %get-tuple-element.16.gain_raw, ...), custom_call_target="tpu_custom_call" | custom-call | tf_op jit(solution)/shard_map/pallas_call | solution.py:607
